TPU v7x, 256 devices: a whole 4x4x8 slice. The times are simulated.
256 devices in a mesh: blk: 32 (over y_lo, z, core), grp: 8 (over x, y_hi).
Axes of the slice: x: 4, y: 4 (y_hi: 2, y_lo: 2; y = y_hi * 2 + y_lo), z: 8, core: 2. Of those that a mesh axis runs over, the one named last changes fastest.
Arguments:
- embeddings: float32 [16384, 1536], P('blk'), may hold values from -0.15 to 0.15
- partner: int32 [16384], P('blk'), may hold values from 0 to 16383, as said below
- inv_temp: int32 [1], replicated, may hold values from 8 to 20
Outputs:
- view_loss: float32 [16384], P('blk')
- grad_embed: float32 [16384, 1536], P('blk', 'grp')
Inputs may be any that keep to these rules, and one draw needn't show every extreme that they name: partner[partner[i]] equals i and partner[i] differs from i for every view i.
All inputs are finite; a program needn't handle non-finite values.
Results may differ from a plain program's by a relative error of at most 0.0052.
Values may be sent and summed in bfloat16 or wider, within the bound.
A program may use at most 64 MiB of HBM per device.

v0:
```python
import jax
import jax.numpy as jnp
from jax import lax
from jax.sharding import PartitionSpec as P


def shards(embeddings, partner, inv_temp):
    temper = inv_temp[0].astype(jnp.float32)
    row_count = embeddings.shape[0]
    feat_width = embeddings.shape[1]
    group_count = lax.axis_size("grp")
    share = row_count // group_count
    feat_share = feat_width // group_count
    my_block = lax.axis_index("blk")
    my_group = lax.axis_index("grp")
    rinv = lax.rsqrt(jnp.sum(embeddings * embeddings, axis=1, keepdims=True) + 1e-06)
    unit = embeddings * rinv
    query = unit.astype(jnp.bfloat16)
    row_ids = my_block * row_count + jnp.arange(row_count, dtype=jnp.int32)
    own_keys = lax.dynamic_slice_in_dim(query, my_group * share, share, 0)

    def block_scores(key_piece):
        positions = jnp.arange(key_piece.shape[0], dtype=jnp.int32)
        key_ids = positions // share * row_count + my_group * share + positions % share
        scores = temper * lax.dot_general(
            query, key_piece, (((1,), (1,)), ((), ())), preferred_element_type=jnp.float32
        )
        expon = jnp.where(row_ids[:, None] != key_ids[None, :], jnp.exp(scores - temper), 0.0)
        is_mate = partner[:, None] == key_ids[None, :]
        return (scores, expon, is_mate)

    scores, expon, is_mate = block_scores(lax.all_gather(own_keys, "blk", axis=0, tiled=True))
    sums, pos = lax.psum(
        (jnp.sum(expon, axis=1), jnp.sum(jnp.where(is_mate, scores, 0.0), axis=1)), "grp"
    )
    view_loss = temper + jnp.log(sums) - pos
    inverse = 1.0 / sums
    key_inverse = lax.all_gather(
        lax.dynamic_slice_in_dim(inverse, my_group * share, share, 0), "blk", axis=0, tiled=True
    )
    key_piece = lax.all_gather(own_keys, "blk", axis=0, tiled=True)
    scores, expon, is_mate = block_scores(key_piece)
    weights = expon * (inverse[:, None] + key_inverse[None, :]) - jnp.where(is_mate, 2.0, 0.0)
    summed = jnp.dot(weights.astype(jnp.bfloat16), key_piece, preferred_element_type=jnp.float32)
    scaled = temper * summed
    full_grad = lax.psum(scaled, "grp")
    inner = jnp.sum(unit * full_grad, axis=1, keepdims=True)
    grad_full = (full_grad - unit * inner) * rinv
    grad_embed = lax.dynamic_slice_in_dim(grad_full, my_group * feat_share, feat_share, 1)
    return (view_loss, grad_embed)


def solution(mesh):
    in_specs = (P("blk", None), P("blk"), P())
    out_specs = (P("blk"), P("blk", "grp"))
    return jax.shard_map(shards, mesh=mesh, in_specs=in_specs, out_specs=out_specs, check_vma=False)
```

profile of v0, /device:TPU:1, one launch (start us, length us, event | category | flops | bytes accessed | tf_op | source)
XLA Modules:
  0.0 341.2 jit_solution(4015748186865706623)
XLA Ops:
  7.2 0.0 all-gather.2.cloned.1.call-start
  7.2 0.0 copy-start
  7.2 2.3 multiply_reduce_fusion.1
  9.6 0.5 copy-done
  10.1 0.0 copy-start.2
  10.1 0.0 copy-start.1
  10.1 1.5 fusion.26
  11.6 1.6 constant_dynamic-slice_fusion
  13.2 0.0 all-gather.2.cloned.1.call-update
  13.2 0.0 all-reduce.4.cloned.1.call-start
  13.9 0.0 copy-done.2
  13.9 0.6 dynamic-slice
  15.2 72.6 %all-gather.2.cloned.1.call-done = bf16[2048,1536]{1,0:T(8,128)(2,1)} async-done(((bf16[64,1536]{1,0:T(8,128)(2,1)}), bf16[2048,1536]{1,0:T(8,128)(2,1)}) %all-gather.2.cloned.1.call-update) | async-done | bytes 6291472 | tf_op jit(solution)/shard_map/all_gather | solution.py:32
  87.8 0.0 copy-done.1
  87.8 9.1 %fusion.3 = (f32[512]{0:T(512)S(1)}, f32[512]{0:T(512)S(1)}, f32[512,2048]{1,0:T(8,128)}) fusion(f32[]{:T(128)} %bitcast, s32[2048]{0:T(1024)S(1)} %fusion.22, s32[512]{0:T(512)S(1)} %iota_add_fusion, s32[512]{0:T(512)S(1)} %copy-done.1, bf16[512,1536]{1,0:T(8,128)(2,1)} %get-tuple-element.8, bf16[2048,1536]{1,0:T(8,128)(2,1)} %all-gather.2.cloned.1.call-done), kind=kOutput, calls=%fused_computation.9 | convolution fusion | flops 3229613056 | bytes 12075012 | tf_op jit(solution)/shard_map/dot_general | solution.py:25
  96.9 20.3 %all-reduce.1 = (f32[512]{0:T(512)S(1)}, f32[512]{0:T(512)S(1)}) all-reduce(f32[512]{0:T(512)S(1)} %get-tuple-element.5, f32[512]{0:T(512)S(1)} %get-tuple-element.4), channel_id=1, replica_groups=mesh['blk'=32,'grp'=8] {'grp'}, use_global_device_ids=true, to_apply=%region_4.5 | all-reduce | flops 1024 | bytes 8192 | tf_op jit(solution)/shard_map/psum | solution.py:33
  117.2 0.6 broadcast_divide_fusion
  117.8 0.2 dynamic-slice_dynamic-update-slice_fusion
  117.9 57.3 %all-reduce = f32[2048]{0:T(1024)S(1)} all-reduce(f32[2048]{0:T(1024)S(1)} %dynamic-slice_dynamic-update-slice_fusion), channel_id=1, replica_groups=mesh['blk'=32,'grp'=8] {'blk'}, use_global_device_ids=true, to_apply=%add | all-reduce | flops 2048 | bytes 16384
  175.2 9.8 %convolution_multiply_fusion = f32[512,1536]{1,0:T(8,128)} fusion(bf16[2048,1536]{1,0:T(8,128)(2,1)} %all-gather.2.cloned.1.call-done, f32[512,2048]{1,0:T(8,128)} %get-tuple-element.12, f32[2048]{0:T(1024)S(1)} %all-reduce, f32[512]{0:T(512)S(1)} %get-tuple-element.10, f32[]{:T(128)} %bitcast, s32[2048]{0:T(1024)S(1)} %fusion.22, s32[512]{0:T(512)S(1)} %copy-done.1, ...), kind=kOutput, calls=%fused_computation.6 | convolution fusion | flops 3232497664 | bytes 13654020 | tf_op jit(solution)/shard_map/dot_general | solution.py:44
  185.0 0.0 all-reduce.4.cloned.1.call-update
  185.1 142.4 %all-reduce.4.cloned.1.call-done = f32[512,1536]{1,0:T(8,128)} async-done(((f32[512,1536]{1,0:T(8,128)}), f32[512,1536]{1,0:T(8,128)}) %all-reduce.4.cloned.1.call-update) | async-done | bytes 3145744 | tf_op jit(solution)/shard_map/psum | solution.py:46
  327.5 2.5 multiply_reduce_fusion
  329.9 2.4 fusion.13
  332.4 2.0 copy.5
  (4 shorter events, 0.0 us)
Async XLA Ops:
  7.2 80.6 %all-gather.2.cloned.1.call-start = ((), (), s32[]{:S(2)}) async-start(), calls=%async_computation | async-start | bytes 6488064 | tf_op jit(solution)/shard_map/all_gather | solution.py:32
  7.2 2.8 copy-start
  10.1 3.9 %copy-start.2 = (u32[256]{0:T(256)S(1)}, u32[256]{0:T(256)}, u32[]{:S(2)}) copy-start(u32[256]{0:T(256)} %constant.63) | copy-start | bytes 3076
  10.1 77.7 %copy-start.1 = (s32[512]{0:T(512)S(1)}, s32[512]{0:T(512)}, u32[]{:S(2)}) copy-start(s32[512]{0:T(512)} %param.4) | copy-start | bytes 6148
  13.2 314.2 %all-reduce.4.cloned.1.call-start = ((), (), s32[]{:S(2)}) async-start(), calls=%async_computation.1 | async-start | bytes 6291456 | tf_op jit(solution)/shard_map/psum | solution.py:46
Sparse Core Ops, SparseCore 0:
  13.3 74.4 all-gather.1
  185.2 142.2 all-reduce.3
where the time goes:
time: 343 us; the launch traced here: 341 us
  waiting for transfers between devices  215 us (63%)
  blocking collectives  77.6 us (23%)
  matrix products  18.9 us (6%)
  between operations  15.4 us (4%)
  other arithmetic  9.35 us (3%)
  local copies, waits for them, and re-layouts  4.84 us (1%)
    psum x1, waiting for transfers between devices, shards(): full_grad = lax.psum(scaled, 'grp')  142 us
    all_gather x1, waiting for transfers between devices, shards(): lax.all_gather(own_keys, 'blk', axis=0, tiled=True)  72.6 us
    unnamed x1, blocking collectives  57.3 us
    psum x1, blocking collectives, shards(): lax.psum((jnp.sum(expon, axis=1), jnp.sum(jnp.where(is_mate, scores, 0.0)...  20.3 us
    dot_general x1, matrix products, shards(): jnp.dot(weights.astype(jnp.bfloat16), key_piece, preferred_element_type=j...  9.8 us
    dot_general x1, matrix products, block_scores(): lax.dot_general(query, key_piece, (((1,), (1,)), ((), ())), preferred_ele...  9.06 us
  transfers between devices with their start and end apart: 2, of which 2 were waited for; matrix products, arithmetic and copies ran while one was open for 0% of the time, Pallas kernels for 0%

commit v1 on v0

v1 whole, which is shorter than its diff:
```python
import functools

import jax
import jax.numpy as jnp
from jax import lax
from jax.experimental import pallas as pl
from jax.experimental.pallas import tpu as pltpu
from jax.sharding import PartitionSpec as P

MESH = pl.DeviceIdType.MESH
ROWS = 512
FEATS = 1536
SEG = 32
CHUNK = 256
KEYS = 2048
QUART = 384
HALF = 256


def slot(dist, side, other_y, other_core, part):
    if dist in (0, 4):
        return (0 if dist == 0 else 7 * CHUNK) + 128 * other_y + 64 * other_core + 32 * part
    return (2 * dist - 1 + other_y) * CHUNK + 128 * other_core + 64 * side + 32 * part


def kernel(
    temp_ref, partner_ref, emb_hbm, loss_ref, grad_ref,
    emb, query, rinv, keys, scores, expon, weights, sum_acc, pos_acc, row_inv, mate_col,
    stat_out, stat_in, inv_in, inv_sib, far_buf, near_buf, hold_top, hold_bot, relay_in, side_in, acc, cross_out, cross_in,
    load_sem, ag_send, ag_recv, stat_sem, inv_sem, rs_send, rs_recv,
):
    blk = lax.axis_index("blk")
    grp = lax.axis_index("grp")
    ylo = lax.div(blk, 16)
    z = lax.rem(lax.div(blk, 2), 8)
    core = lax.rem(blk, 2)
    x = lax.div(grp, 2)
    yhi = lax.rem(grp, 2)
    y = yhi * 2 + ylo
    part_a = yhi
    part_b = lax.rem(yhi + ylo, 2)

    def device(x_, y_, z_, core_):
        return (lax.rem(y_, 2) * 16 + z_ * 2 + core_, x_ * 2 + lax.div(y_, 2))

    z_right = device(x, y, lax.rem(z + 1, 8), core)
    z_left = device(x, y, lax.rem(z + 7, 8), core)
    y_a = y + 1 - 2 * ylo
    y_b = 3 - y
    dev_a = device(x, y_a, z, core)
    dev_b = device(x, y_b, z, core)
    sib = device(x, y, z, 1 - core)
    x_right = device(lax.rem(x + 1, 4), y, z, core)
    x_left = device(lax.rem(x + 3, 4), y, z, core)
    dev_cross = device(x, lax.rem(y + 2, 4), z, core)
    peers = [(blk, lax.rem(grp + r, 8)) for r in range(1, 8)]

    loads = []
    for i in range(4):
        rows = pl.ds(pl.multiple_of(lax.rem(x + i, 4) * 128, 128), 128)
        copy = pltpu.make_async_copy(emb_hbm.at[rows], emb.at[rows], load_sem.at[i])
        copy.start()
        loads.append(copy)

    barrier = pltpu.get_barrier_semaphore()
    greeted = [z_right, z_left, dev_a, dev_b, sib] + peers
    for target in greeted:
        pl.semaphore_signal(barrier, inc=1, device_id=target, device_id_type=MESH)

    temper = temp_ref[0].astype(jnp.float32)

    def normalize(i):
        loads[i].wait()
        first = lax.rem(x + i, 4) * 128

        def step(j, carry):
            rows = pl.ds(pl.multiple_of(first + j * 32, 32), 32)
            e = emb[rows, :]
            r = lax.rsqrt(jnp.sum(e * e, axis=1, keepdims=True) + 1e-06)
            query[rows, :] = (e * r).astype(jnp.bfloat16)
            rinv[rows, :] = jnp.broadcast_to(r, (32, 128))
            return carry

        lax.fori_loop(0, 4, step, 0)

    normalize(0)
    rows_a = pl.ds(pl.multiple_of(x * 128 + part_a * 32, 32), SEG)
    rows_b = pl.ds(pl.multiple_of(x * 128 + 64 + part_b * 32, 32), SEG)
    keys[0:SEG, :] = query[rows_a, :]
    keys[SEG : 2 * SEG, :] = query[rows_b, :]

    pl.semaphore_wait(barrier, len(greeted))

    messages = []

    def message(src, dst, rows, target):
        i = len(messages)
        copy = pltpu.make_async_remote_copy(
            src_ref=keys.at[pl.ds(src, rows)],
            dst_ref=keys.at[pl.ds(dst, rows)],
            send_sem=ag_send.at[i],
            recv_sem=ag_recv.at[i],
            device_id=target,
            device_id_type=MESH,
        )
        messages.append(copy)
        return copy

    ring, across, twin = {}, {}, {}
    for dist in range(1, 5):
        for part in (0, 1):
            for side in (0, 1):
                if dist == 4 and side != part:
                    continue
                src = slot(dist - 1, side, 0, 0, part)
                dst = slot(dist, side, 0, 0, part)
                ring[side, dist, part] = message(src, dst, SEG, z_right if side == 0 else z_left)
    for dist in range(5):
        for side in (0, 1):
            if dist in (0, 4) and side == 1:
                continue
            for part in (0, 1):
                across[side, dist, part] = message(
                    slot(dist, side, 0, 0, part), slot(dist, side, 1, 0, part), SEG, dev_a if part == 0 else dev_b
                )
            for other in (0, 1):
                twin[side, dist, other] = message(
                    slot(dist, side, other, 0, 0), slot(dist, side, other, 1, 0), 2 * SEG, sib
                )

    lane = lax.broadcasted_iota(jnp.int32, (1, CHUNK), 1)

    def key_ids(chunk):
        if chunk in (0, 7):
            zk = lax.rem(z + (0 if chunk == 0 else 4), 8)
            yk = jnp.where(lane < 128, ylo, 1 - ylo)
            ck = jnp.where(lane % 128 < 64, core, 1 - core)
        else:
            dist = (chunk + 1) // 2
            zk = jnp.where(lane % 128 < 64, lax.rem(z + 8 - dist, 8), lax.rem(z + dist, 8))
            yk = ylo if chunk % 2 == 1 else 1 - ylo
            ck = jnp.where(lane < 128, core, 1 - core)
        within = jnp.where(lane % 64 < 32, part_a * 32, part_b * 32 + 64) + lane % 32
        return (((yk * 8 + zk) * 2 + ck) * ROWS + x * 128 + within).astype(jnp.float32)

    def score_chunk(chunk):
        cols = slice(chunk * CHUNK, (chunk + 1) * CHUNK)
        ids = key_ids(chunk)

        def step(j, carry):
            rows = pl.ds(pl.multiple_of(j * HALF, HALF), HALF)
            s = temper * lax.dot_general(
                query[rows, :], keys[cols, :], (((1,), (1,)), ((), ())), preferred_element_type=jnp.float32
            )
            e = jnp.exp(s - temper)
            if chunk == 0:
                own = lax.broadcasted_iota(jnp.int32, (HALF, CHUNK), 0) + (blk * ROWS + j * HALF)
                e = jnp.where(own.astype(jnp.float32) == ids, 0.0, e)
            mate = mate_col[rows, :]
            mate = jnp.concatenate([mate, mate], axis=1)
            p = jnp.where(mate == ids, s, 0.0)
            scores[rows, cols] = s
            expon[rows, cols] = e
            if chunk == 0:
                sum_acc[rows, :] = e[:, :128] + e[:, 128:]
                pos_acc[rows, :] = p[:, :128] + p[:, 128:]
            else:
                sum_acc[rows, :] += e[:, :128] + e[:, 128:]
                pos_acc[rows, :] += p[:, :128] + p[:, 128:]
            return carry

        lax.fori_loop(0, ROWS // HALF, step, 0)

    for part in (0, 1):
        for side in (0, 1):
            ring[side, 1, part].start()
    for part in (0, 1):
        across[0, 0, part].start()
    twin[0, 0, 0].start()
    mate_row = jnp.broadcast_to(partner_ref[...].astype(jnp.float32), (128, ROWS))
    mate_col[...] = mate_row.T
    for i in range(1, 4):
        normalize(i)

    def finish_across(dist):
        for side in ((0,) if dist in (0, 4) else (0, 1)):
            for part in (0, 1):
                across[side, dist, part].wait_recv()
            twin[side, dist, 1].start()

    def finish_twin(dist, other):
        for side in ((0,) if dist in (0, 4) else (0, 1)):
            twin[side, dist, other].wait_recv()

    for dist in range(1, 4):
        for part in (0, 1):
            for side in (0, 1):
                ring[side, dist, part].wait_recv()
                if dist < 3 or side == part:
                    ring[side, dist + 1, part].start()
                across[side, dist, part].start()
                if part == 1:
                    twin[side, dist, 0].start()
            if part == 0:
                finish_across(dist - 1)
                if dist > 1:
                    finish_twin(dist - 1, 0)
                    score_chunk(2 * (dist - 1) - 1)
            else:
                finish_twin(dist - 1, 1)
                if dist == 1:
                    finish_twin(0, 0)
                    score_chunk(0)
                else:
                    score_chunk(2 * (dist - 1))
    for part in (0, 1):
        ring[part, 4, part].wait_recv()
        across[0, 4, part].start()
    twin[0, 4, 0].start()
    finish_across(3)
    finish_twin(3, 0)
    score_chunk(5)
    finish_twin(3, 1)
    score_chunk(6)
    finish_across(4)
    finish_twin(4, 0)
    finish_twin(4, 1)
    score_chunk(7)

    stat_out[0:1, :] = jnp.sum(sum_acc[...].T, axis=0, keepdims=True)
    stat_out[1:2, :] = jnp.sum(pos_acc[...].T, axis=0, keepdims=True)
    for r in range(1, 8):
        pltpu.make_async_remote_copy(
            src_ref=stat_out,
            dst_ref=stat_in.at[r],
            send_sem=stat_sem.at[0],
            recv_sem=stat_sem.at[1],
            device_id=peers[r - 1],
            device_id_type=MESH,
        ).start()
    for copy in messages:
        copy.wait_send()
    stat_all = pltpu.make_async_remote_copy(
        src_ref=stat_in.at[pl.ds(1, 7)],
        dst_ref=stat_in.at[pl.ds(1, 7)],
        send_sem=stat_sem.at[0],
        recv_sem=stat_sem.at[1],
        device_id=peers[0],
        device_id_type=MESH,
    )
    stat_all.wait_recv()
    total = stat_out[...]
    for r in range(1, 8):
        total = total + stat_in[r]
    sums = total[0:1, :]
    inverse = 1.0 / sums
    loss_ref[...] = temper + jnp.log(sums) - total[1:2, :]

    row_inv[0:128, :] = jnp.broadcast_to(inverse[:, 0:128], (128, 128)).T
    row_inv[128:256, :] = jnp.broadcast_to(inverse[:, 128:256], (128, 128)).T
    row_inv[256:384, :] = jnp.broadcast_to(inverse[:, 256:384], (128, 128)).T
    row_inv[384:512, :] = jnp.broadcast_to(inverse[:, 384:512], (128, 128)).T
    tile = jnp.where(x == 0, inverse[:, 0:128], inverse[:, 128:256])
    tile = jnp.where(x == 2, inverse[:, 256:384], tile)
    tile = jnp.where(x == 3, inverse[:, 384:512], tile)
    lane1 = lax.broadcasted_iota(jnp.int32, (1, 128), 1)
    by32 = jnp.concatenate([tile[:, 32:], tile[:, :32]], axis=1)
    by64 = jnp.concatenate([tile[:, 64:], tile[:, :64]], axis=1)
    first = jnp.where(part_a == 0, tile, by32)
    second = jnp.where(part_b == 0, by32, by64)
    pair = jnp.where(lane1 < 32, first, second)
    pair = jnp.where(lane1 < 64, pair, jnp.concatenate([pair[:, 64:], pair[:, :64]], axis=1))
    inv_in[0] = pair
    inv_targets = [(dz, device(x, y, lax.rem(z + dz, 8), core)) for dz in range(1, 8)]
    inv_targets += [(8 + dz, device(x, y_a, lax.rem(z + dz, 8), core)) for dz in range(8)]
    inv_targets += [(16 + dz, device(x, y_b, lax.rem(z + dz, 8), core)) for dz in range(8)]
    for i, target in inv_targets:
        pltpu.make_async_remote_copy(
            src_ref=inv_in.at[0],
            dst_ref=inv_in.at[i],
            send_sem=inv_sem.at[0],
            recv_sem=inv_sem.at[1],
            device_id=target,
            device_id_type=MESH,
        ).start()
    stat_all.wait_send()
    inv_all = pltpu.make_async_remote_copy(
        src_ref=inv_in.at[pl.ds(1, 23)],
        dst_ref=inv_in.at[pl.ds(1, 23)],
        send_sem=inv_sem.at[0],
        recv_sem=inv_sem.at[1],
        device_id=sib,
        device_id_type=MESH,
    )
    inv_all.wait_recv()
    inv_twin = pltpu.make_async_remote_copy(
        src_ref=inv_in,
        dst_ref=inv_sib,
        send_sem=inv_sem.at[2],
        recv_sem=inv_sem.at[3],
        device_id=sib,
        device_id_type=MESH,
    )
    inv_twin.start()
    inv_twin.wait_recv()

    def key_inv(chunk):
        low = lane1 < 64
        is_a = lane1 % 64 < 32

        def of(ref, dz, other_y):
            if other_y == 0:
                return ref[dz]
            return jnp.where(is_a, ref[8 + dz], ref[16 + dz])

        if chunk in (0, 7):
            dz = 0 if chunk == 0 else 4
            tiles = [jnp.where(low, of(inv_in, dz, o), of(inv_sib, dz, o)) for o in (0, 1)]
        else:
            dist = (chunk + 1) // 2
            o = 0 if chunk % 2 == 1 else 1
            tiles = [jnp.where(low, of(ref, dist, o), of(ref, 8 - dist, o)) for ref in (inv_in, inv_sib)]
        return jnp.concatenate(tiles, axis=1)

    for chunk in range(8):
        cols = slice(chunk * CHUNK, (chunk + 1) * CHUNK)
        ids = key_ids(chunk)
        col_inv = key_inv(chunk)

        def weigh(j, carry, cols=cols, ids=ids, col_inv=col_inv, chunk=chunk):
            rows = pl.ds(pl.multiple_of(j * 64, 64), 64)
            ri = row_inv[rows, :]
            mate = mate_col[rows, :]
            w = expon[rows, cols] * (jnp.concatenate([ri, ri], axis=1) + col_inv)
            w = w - jnp.where(jnp.concatenate([mate, mate], axis=1) == ids, 2.0, 0.0)
            w = w.astype(jnp.bfloat16)
            weights[rows, cols] = w
            inner = w.astype(jnp.float32) * scores[rows, cols]
            inner = inner[:, :128] + inner[:, 128:]
            if chunk == 0:
                sum_acc[rows, :] = inner
            else:
                sum_acc[rows, :] += inner
            return carry

        lax.fori_loop(0, ROWS // 64, weigh, 0)

    def coefs(j, carry):
        rows = pl.ds(pl.multiple_of(j * 64, 64), 64)
        r = rinv[rows, :]
        inner = jnp.sum(sum_acc[rows, :], axis=1, keepdims=True)
        pos_acc[rows, :] = r * r * inner
        sum_acc[rows, :] = r * temper
        return carry

    lax.fori_loop(0, ROWS // 64, coefs, 0)

    def grad_piece(ahead, top):
        cols = pl.ds(pl.multiple_of(lax.rem(x + ahead, 4) * QUART, QUART), QUART)
        rows = pl.ds(0 if top else HALF, HALF)
        d = jnp.dot(weights[rows, :], keys[:, cols], preferred_element_type=jnp.float32)
        u = sum_acc[rows, :]
        v = pos_acc[rows, :]
        return d * jnp.concatenate([u] * 3, axis=1) - emb[rows, cols] * jnp.concatenate([v] * 3, axis=1)

    def rs_message(i, src, dst, target):
        return pltpu.make_async_remote_copy(
            src_ref=src, dst_ref=dst, send_sem=rs_send.at[i], recv_sem=rs_recv.at[i],
            device_id=target, device_id_type=MESH,
        )

    far_right = rs_message(0, far_buf.at[0], relay_in.at[0], x_right)
    far_left = rs_message(1, far_buf.at[1], relay_in.at[1], x_left)
    right_bot = rs_message(2, near_buf.at[0], side_in.at[0], x_right)
    left_top = rs_message(3, near_buf.at[1], side_in.at[1], x_left)
    right_top = rs_message(4, near_buf.at[2], side_in.at[2], x_right)
    left_bot = rs_message(5, near_buf.at[3], side_in.at[3], x_left)
    cross = rs_message(6, cross_out, cross_in, dev_cross)

    far_buf[0] = grad_piece(2, True).astype(jnp.bfloat16)
    far_right.start()
    far_buf[1] = grad_piece(2, False).astype(jnp.bfloat16)
    far_left.start()
    near_buf[0] = grad_piece(1, False).astype(jnp.bfloat16)
    right_bot.start()
    near_buf[1] = grad_piece(3, True).astype(jnp.bfloat16)
    left_top.start()
    hold_top[...] = grad_piece(1, True)
    hold_bot[...] = grad_piece(3, False)
    far_right.wait_recv()
    near_buf[2] = (hold_top[...] + relay_in[0].astype(jnp.float32)).astype(jnp.bfloat16)
    right_top.start()
    far_left.wait_recv()
    near_buf[3] = (hold_bot[...] + relay_in[1].astype(jnp.float32)).astype(jnp.bfloat16)
    left_bot.start()
    acc[0:HALF, :] = grad_piece(0, True)
    acc[HALF:ROWS, :] = grad_piece(0, False)
    right_bot.wait_recv()
    left_top.wait_recv()
    acc[HALF:ROWS, :] += side_in[0].astype(jnp.float32)
    acc[0:HALF, :] += side_in[1].astype(jnp.float32)
    right_top.wait_recv()
    left_bot.wait_recv()
    acc[0:HALF, :] += side_in[2].astype(jnp.float32)
    acc[HALF:ROWS, :] += side_in[3].astype(jnp.float32)
    whole = acc[...]
    first_half, second_half = whole[:, :192], whole[:, 192:]
    cross_out[...] = jnp.where(yhi == 0, second_half, first_half).astype(jnp.bfloat16)
    cross.start()
    grad_ref[...] = jnp.where(yhi == 0, first_half, second_half)
    cross.wait_recv()
    grad_ref[...] += cross_in[...].astype(jnp.float32)
    inv_all.wait_send()
    inv_twin.wait_send()
    for copy in (far_right, far_left, right_bot, left_top, right_top, left_bot, cross):
        copy.wait_send()


def shards(embeddings, partner, inv_temp):
    f32, bf16 = jnp.float32, jnp.bfloat16
    vmem = pl.BlockSpec(memory_space=pltpu.VMEM)
    loss, grad = pl.pallas_call(
        kernel,
        out_shape=(jax.ShapeDtypeStruct((1, ROWS), f32), jax.ShapeDtypeStruct((ROWS, 192), f32)),
        in_specs=[pl.BlockSpec(memory_space=pltpu.SMEM), vmem, pl.BlockSpec(memory_space=pl.ANY)],
        out_specs=(vmem, vmem),
        scratch_shapes=[
            pltpu.VMEM((ROWS, FEATS), f32),
            pltpu.VMEM((ROWS, FEATS), bf16),
            pltpu.VMEM((ROWS, 128), f32),
            pltpu.VMEM((KEYS, FEATS), bf16),
            pltpu.VMEM((ROWS, KEYS), f32),
            pltpu.VMEM((ROWS, KEYS), f32),
            pltpu.VMEM((ROWS, KEYS), bf16),
            pltpu.VMEM((ROWS, 128), f32),
            pltpu.VMEM((ROWS, 128), f32),
            pltpu.VMEM((ROWS, 128), f32),
            pltpu.VMEM((ROWS, 128), f32),
            pltpu.VMEM((2, ROWS), f32),
            pltpu.VMEM((8, 2, ROWS), f32),
            pltpu.VMEM((24, 1, 128), f32),
            pltpu.VMEM((24, 1, 128), f32),
            pltpu.VMEM((2, HALF, QUART), bf16),
            pltpu.VMEM((4, HALF, QUART), bf16),
            pltpu.VMEM((HALF, QUART), f32),
            pltpu.VMEM((HALF, QUART), f32),
            pltpu.VMEM((2, HALF, QUART), bf16),
            pltpu.VMEM((4, HALF, QUART), bf16),
            pltpu.VMEM((ROWS, QUART), f32),
            pltpu.VMEM((ROWS, 192), bf16),
            pltpu.VMEM((ROWS, 192), bf16),
            pltpu.SemaphoreType.DMA((4,)),
            pltpu.SemaphoreType.DMA((48,)),
            pltpu.SemaphoreType.DMA((48,)),
            pltpu.SemaphoreType.DMA((2,)),
            pltpu.SemaphoreType.DMA((4,)),
            pltpu.SemaphoreType.DMA((7,)),
            pltpu.SemaphoreType.DMA((7,)),
        ],
        compiler_params=pltpu.CompilerParams(
            collective_id=0, has_side_effects=True, vmem_limit_bytes=48 * 1024 * 1024
        ),
    )(inv_temp, partner.reshape(1, ROWS), embeddings)
    return (loss.reshape(ROWS), grad)


def solution(mesh):
    in_specs = (P("blk", None), P("blk"), P())
    out_specs = (P("blk"), P("blk", "grp"))
    return jax.shard_map(shards, mesh=mesh, in_specs=in_specs, out_specs=out_specs, check_vma=False)
```

time: 343 us -> 83.7 us (0.24)
  waiting for transfers between devices: 215 us -> 0 us
  Pallas kernels: 0 us -> 78.2 us
  blocking collectives: 77.6 us -> 0 us
  matrix products: 18.9 us -> 0 us
  between operations: 15.4 us -> 1.29 us
  other arithmetic: 9.35 us -> 0 us
    psum x1 -> x0, waiting for transfers between devices: 142 us -> none  [shards(): full_grad = lax.psum(scaled, 'grp')]
    pallas_call x0 -> x1, Pallas kernels: none -> 78.2 us  [shards(): pl.pallas_call(kernel, out_shape=(jax.ShapeDtypeStruct((1, ROWS), f32), j...]
    all_gather x1 -> x0, waiting for transfers between devices: 72.6 us -> none  [shards(): lax.all_gather(own_keys, 'blk', axis=0, tiled=True)]
    unnamed x1 -> x0, blocking collectives: 57.3 us -> none
    psum x1 -> x0, blocking collectives: 20.3 us -> none  [shards(): lax.psum((jnp.sum(expon, axis=1), jnp.sum(jnp.where(is_mate, scores, 0.0)...]
    dot_general x2 -> x0, matrix products: 18.9 us -> none  [the longest x1 9.8 us: shards(): jnp.dot(weights.astype(jnp.bfloat16), key_piece, preferred_element_type=j...]
    reduce_sum x2 -> x0, other arithmetic: 4.8 us -> none  [the longest x1 2.48 us: shards(): inner = jnp.sum(unit * full_grad, axis=1, keepdims=True)]
  transfers between devices with their start and end apart: 2 -> 0, of which waited for: 2 -> 0; matrix products, arithmetic and copies ran while one was open for 0% -> 0% of each run, Pallas kernels for 0% -> 0%
where the time goes in v1:
time: 83.7 us; the launch traced here: 83.6 us
  Pallas kernels  78.2 us (93%)
  local copies, waits for them, and re-layouts  4.07 us (5%)
  between operations  1.29 us (2%)
    pallas_call x1, Pallas kernels, shards(): pl.pallas_call(kernel, out_shape=(jax.ShapeDtypeStruct((1, ROWS), f32), j...  78.2 us
    unnamed x6, local copies, waits for them, and re-layouts  4.07 us

profile of v1, /device:TPU:1, one launch (start us, length us, event | category | flops | bytes accessed | tf_op | source)
XLA Modules:
  0.0 83.6 jit_solution(87414845792793899)
XLA Ops:
  1.3 0.0 copy-start
  1.3 1.9 %copy-done = f32[512,1536]{1,0:T(8,128)S(1)} copy-done((f32[512,1536]{1,0:T(8,128)S(1)}, f32[512,1536]{1,0:T(8,128)}, u32[]{:S(2)}) %copy-start) | copy-done | bytes 3145752
  3.2 0.0 copy-start.1
  3.2 0.7 copy-done.1
  3.8 78.2 %shard_map.50 = (f32[1,512]{1,0:T(1,128)S(1)}, f32[512,192]{1,0:T(8,128)S(1)}) custom-call(s32[1]{0:T(128)S(6)} %copy.7.temp_ref, s32[1,512]{1,0:T(1,128)S(1)} %bitcast.2, f32[512,1536]{1,0:T(8,128)S(1)} %copy-done), custom_call_target="tpu_custom_call" | custom-call | tf_op jit(solution)/shard_map/pallas_call | solution.py:422
  82.0 0.9 %copy.5 = f32[512,192]{0,1:T(8,128)} copy(f32[512,192]{1,0:T(8,128)S(1)} %get-tuple-element.7) | data formatting | bytes 786432
  83.0 0.6 copy.8
Async XLA Ops:
  1.3 1.9 %copy-start = (f32[512,1536]{1,0:T(8,128)S(1)}, f32[512,1536]{1,0:T(8,128)}, u32[]{:S(2)}) copy-start(f32[512,1536]{1,0:T(8,128)} %emb_hbm.1) | copy-start | bytes 9437188
  3.2 0.7 copy-start.1

commit v2 on v0

v2 whole, which is shorter than its diff:
```python
import jax
import jax.numpy as jnp
from jax import lax
from jax.experimental import pallas as pl
from jax.experimental.pallas import tpu as pltpu
from jax.sharding import PartitionSpec as P

MESH = pl.DeviceIdType.MESH
ROWS = 512
FEATS = 1536
SUB = 16
CHUNK = 256
KEYS = 2048
QUART = 384
HALF = 256
FORTH = 128


def tile_of(dist, side, other_y):
    if dist in (0, 4):
        return (0 if dist == 0 else 14) + other_y
    return 2 * (2 * dist - 1 + other_y) + side


TILES = {}
for _d in range(5):
    for _s in (0, 1):
        for _o in (0, 1):
            if not (_d in (0, 4) and _s == 1):
                TILES[tile_of(_d, _s, _o)] = (_d, _s, _o)


def slot(dist, side, other_y, other_core, piece):
    return 128 * tile_of(dist, side, other_y) + 64 * other_core + SUB * piece


def turn(v):
    return pltpu.roll(v, 64, axis=1)


def pack(v, mask):
    n = v.shape[0] // 2
    return jnp.where(mask, v[:n], turn(v[n:]))


def unpack(m):
    return jnp.concatenate([m, turn(m)], axis=0)


def kernel(
    temp_ref, partner_ref, emb_hbm, loss_ref, grad_ref,
    emb, query, rinv, keys, scores, expon, weights, sum_acc, pos_acc, row_inv, mate_col,
    stat_out, stat_in, col_out, col_near, col_sum, col_far, key_tot,
    far_buf, near_buf, relay_in, side_in, hold_x, acc, hold_full, hold_half,
    yo_buf, yi_buf, cross_out, cross_in, xo_buf, xi_buf,
    load_sem, ag_send, ag_recv, stat_sem, col_sem, rs_send, rs_recv,
):
    blk = lax.axis_index("blk")
    grp = lax.axis_index("grp")
    ylo = lax.div(blk, 16)
    z = lax.rem(lax.div(blk, 2), 8)
    core = lax.rem(blk, 2)
    x = lax.div(grp, 2)
    yhi = lax.rem(grp, 2)
    y = yhi * 2 + ylo
    part_a = yhi
    part_b = lax.rem(yhi + ylo, 2)

    def device(x_, y_, z_, core_):
        return (lax.rem(y_, 2) * 16 + z_ * 2 + core_, x_ * 2 + lax.div(y_, 2))

    z_right = device(x, y, lax.rem(z + 1, 8), core)
    z_left = device(x, y, lax.rem(z + 7, 8), core)
    y_a = y + 1 - 2 * ylo
    y_b = 3 - y
    dev_a = device(x, y_a, z, core)
    dev_b = device(x, y_b, z, core)
    sib = device(x, y, z, 1 - core)
    x_right = device(lax.rem(x + 1, 4), y, z, core)
    x_left = device(lax.rem(x + 3, 4), y, z, core)
    x_far = device(lax.rem(x + 2, 4), y, z, core)
    dev_cross = device(x, lax.rem(y + 2, 4), z, core)
    peers = [(blk, lax.rem(grp + r, 8)) for r in range(1, 8)]

    barrier = pltpu.get_barrier_semaphore()
    greeted = [z_right, z_left, dev_a, dev_b, sib] + peers
    for target in greeted:
        pl.semaphore_signal(barrier, inc=1, device_id=target, device_id_type=MESH)

    loads = []
    for i in range(4):
        rows = pl.ds(pl.multiple_of(lax.rem(x + i, 4) * 128, 128), 128)
        copy = pltpu.make_async_copy(emb_hbm.at[rows], emb.at[rows], load_sem.at[i])
        copy.start()
        loads.append(copy)

    temper = temp_ref[0].astype(jnp.float32)

    def unit_rows(rows):
        e = emb[rows, :]
        r = lax.rsqrt(jnp.sum(e * e, axis=1, keepdims=True) + 1e-06)
        return (e * r).astype(jnp.bfloat16), r

    def normalize(i):
        first = lax.rem(x + i, 4) * 128

        def step(j, carry):
            for k in range(4):
                rows = pl.ds(pl.multiple_of(first + j * 64 + k * SUB, SUB), SUB)
                q, r = unit_rows(rows)
                query[rows, :] = q
                rinv[rows, :] = jnp.broadcast_to(r, (SUB, 128))
            return carry

        lax.fori_loop(0, 2, step, 0)

    loads[0].wait()
    for piece in range(4):
        first = x * 128 + (part_a * 32 if piece < 2 else 64 + part_b * 32) + SUB * (piece % 2)
        q, _ = unit_rows(pl.ds(pl.multiple_of(first, SUB), SUB))
        keys[SUB * piece : SUB * (piece + 1), :] = q

    pl.semaphore_wait(barrier, len(greeted))

    messages = []

    def message(src, dst, rows, target):
        i = len(messages)
        copy = pltpu.make_async_remote_copy(
            src_ref=keys.at[pl.ds(src, rows)],
            dst_ref=keys.at[pl.ds(dst, rows)],
            send_sem=ag_send.at[i],
            recv_sem=ag_recv.at[i],
            device_id=target,
            device_id_type=MESH,
        )
        messages.append(copy)
        return copy

    ring, across, twin = {}, {}, {}
    for dist in range(1, 5):
        for piece in range(4):
            for side in (0, 1):
                if dist == 4 and side != piece // 2:
                    continue
                src = slot(dist - 1, 0 if dist == 1 else side, 0, 0, piece)
                dst = slot(dist, 0 if dist == 4 else side, 0, 0, piece)
                ring[side, dist, piece] = message(src, dst, SUB, z_right if side == 0 else z_left)
    for dist in range(5):
        for side in (0, 1):
            if dist in (0, 4) and side == 1:
                continue
            for piece in range(4):
                across[side, dist, piece] = message(
                    slot(dist, side, 0, 0, piece), slot(dist, side, 1, 0, piece), SUB, dev_a if piece < 2 else dev_b
                )
            for other in (0, 1):
                twin[side, dist, other] = message(
                    slot(dist, side, other, 0, 0), slot(dist, side, other, 1, 0), 4 * SUB, sib
                )

    lane = lax.broadcasted_iota(jnp.int32, (1, 128), 1)

    def tile_place(tile):
        dist, side, other = TILES[tile]
        return lax.rem(z + (8 - dist if side == 0 else dist), 8), other

    def key_ids(chunk):
        ids = []
        for tile in (2 * chunk, 2 * chunk + 1):
            zk, other = tile_place(tile)
            yk = ylo if other == 0 else 1 - ylo
            ck = jnp.where(lane < 64, core, 1 - core)
            within = jnp.where(lane % 64 < 32, part_a * 32, part_b * 32 + 64) + lane % 32
            ids.append((((yk * 8 + zk) * 2 + ck) * ROWS + x * 128 + within).astype(jnp.float32))
        return jnp.concatenate(ids, axis=1)

    def score_chunk(chunk):
        cols = slice(chunk * CHUNK, (chunk + 1) * CHUNK)
        ids = key_ids(chunk)

        def step(j, carry):
            rows = pl.ds(pl.multiple_of(j * HALF, HALF), HALF)
            s = temper * lax.dot_general(
                query[rows, :], keys[cols, :], (((1,), (1,)), ((), ())), preferred_element_type=jnp.float32
            )
            e = jnp.exp(s - temper)
            if chunk == 0:
                own = lax.broadcasted_iota(jnp.int32, (HALF, CHUNK), 0) + (blk * ROWS + j * HALF)
                e = jnp.where(own.astype(jnp.float32) == ids, 0.0, e)
            mate = mate_col[rows, :]
            mate = jnp.concatenate([mate, mate], axis=1)
            p = jnp.where(mate == ids, s, 0.0)
            scores[rows, cols] = s
            expon[rows, cols] = e
            if chunk == 0:
                sum_acc[rows, :] = e[:, :128] + e[:, 128:]
                pos_acc[rows, :] = p[:, :128] + p[:, 128:]
            else:
                sum_acc[rows, :] += e[:, :128] + e[:, 128:]
                pos_acc[rows, :] += p[:, :128] + p[:, 128:]
            return carry + jnp.sum(e, axis=0, keepdims=True)

        total = lax.fori_loop(0, ROWS // HALF, step, jnp.zeros((1, CHUNK), jnp.float32))
        for i in (0, 1):
            zk, other = tile_place(2 * chunk + i)
            col_out[pl.ds(other * 8 + zk, 1), :] = total[:, 128 * i : 128 * (i + 1)]

    for piece in range(4):
        for side in (0, 1):
            ring[side, 1, piece].start()
        across[0, 0, piece].start()
    twin[0, 0, 0].start()
    normalize(0)
    loads[1].wait()
    normalize(1)

    def sides(dist):
        return (0,) if dist in (0, 4) else (0, 1)

    def finish_across(dist):
        for side in sides(dist):
            for piece in range(4):
                across[side, dist, piece].wait_recv()
            twin[side, dist, 1].start()

    def finish_twin(dist, other):
        for side in sides(dist):
            twin[side, dist, other].wait_recv()

    for dist in range(1, 4):
        for piece in range(4):
            for side in (0, 1):
                ring[side, dist, piece].wait_recv()
                if dist < 3 or side == piece // 2:
                    ring[side, dist + 1, piece].start()
                across[side, dist, piece].start()
                if piece == 3:
                    twin[side, dist, 0].start()
            if dist == 1:
                if piece == 0:
                    loads[2].wait()
                    normalize(2)
                elif piece == 1:
                    loads[3].wait()
                    normalize(3)
                    mate_row = jnp.broadcast_to(partner_ref[...].astype(jnp.float32), (128, ROWS))
                    mate_col[...] = mate_row.T
                elif piece == 2:
                    finish_across(0)
                else:
                    finish_twin(0, 0)
                    finish_twin(0, 1)
                    score_chunk(0)
            else:
                if piece == 0:
                    finish_twin(dist - 1, 0)
                    score_chunk(2 * (dist - 1) - 1)
                elif piece == 1:
                    finish_across(dist - 1)
                elif piece == 2:
                    finish_twin(dist - 1, 1)
                    score_chunk(2 * (dist - 1))
    for piece in (0, 2, 1, 3):
        ring[piece // 2, 4, piece].wait_recv()
        across[0, 4, piece].start()
    twin[0, 4, 0].start()
    finish_twin(3, 0)
    score_chunk(5)
    finish_across(3)
    finish_twin(3, 1)
    score_chunk(6)
    finish_across(4)
    finish_twin(4, 0)
    finish_twin(4, 1)
    score_chunk(7)

    def small(src, dst, sems, i, target):
        return pltpu.make_async_remote_copy(
            src_ref=src, dst_ref=dst, send_sem=sems.at[i], recv_sem=sems.at[i + 1],
            device_id=target, device_id_type=MESH,
        )

    near_targets = [sib, dev_a, dev_b, device(x, y_a, z, 1 - core), device(x, y_b, z, 1 - core)]
    for i, target in enumerate(near_targets):
        small(col_out, col_near.at[i], col_sem, 0, target).start()
    stat_out[0:1, :] = jnp.sum(sum_acc[...].T, axis=0, keepdims=True)
    stat_out[1:2, :] = jnp.sum(pos_acc[...].T, axis=0, keepdims=True)
    for r in range(1, 8):
        small(stat_out, stat_in.at[r], stat_sem, 0, peers[r - 1]).start()
    near_all = small(col_near, col_near, col_sem, 0, sib)
    near_all.wait_recv()
    is_a = lax.broadcasted_iota(jnp.int32, (16, 128), 1) % 64 < 32

    def flip(v):
        return jnp.concatenate([v[8:], v[:8]], axis=0)

    over_a = flip(col_near[1] + turn(col_near[3]))
    over_b = flip(col_near[2] + turn(col_near[4]))
    col_sum[...] = col_out[...] + turn(col_near[0]) + jnp.where(is_a, over_a, over_b)
    for dz in range(1, 8):
        small(col_sum, col_far.at[dz], col_sem, 2, device(x, y, lax.rem(z + dz, 8), core)).start()
    for copy in messages:
        copy.wait_send()
    stat_all = small(stat_in.at[pl.ds(1, 7)], stat_in.at[pl.ds(1, 7)], stat_sem, 0, peers[0])
    stat_all.wait_recv()
    total = stat_out[...]
    for r in range(1, 8):
        total = total + stat_in[r]
    sums = total[0:1, :]
    inverse = 1.0 / sums
    loss_ref[...] = temper + jnp.log(sums) - total[1:2, :]
    for i in range(4):
        part = slice(128 * i, 128 * (i + 1))
        row_inv[part, :] = jnp.broadcast_to(inverse[:, part], (128, 128)).T
    far_all = small(col_far.at[pl.ds(1, 7)], col_far.at[pl.ds(1, 7)], col_sem, 2, z_right)
    far_all.wait_recv()
    col_total = col_sum[...]
    for dz in range(1, 8):
        col_total = col_total + col_far[dz]
    key_tot[...] = 1.0 / col_total

    def weigh_rows(first):
        for chunk in range(8):
            cols = slice(chunk * CHUNK, (chunk + 1) * CHUNK)
            ids = key_ids(chunk)
            inv = []
            for tile in (2 * chunk, 2 * chunk + 1):
                zk, other = tile_place(tile)
                inv.append(key_tot[pl.ds(other * 8 + zk, 1), :])
            col_inv = jnp.concatenate(inv, axis=1)

            def weigh(j, carry, cols=cols, ids=ids, col_inv=col_inv, chunk=chunk):
                rows = pl.ds(pl.multiple_of(first + j * 64, 64), 64)
                ri = row_inv[rows, :]
                mate = mate_col[rows, :]
                w = expon[rows, cols] * (jnp.concatenate([ri, ri], axis=1) + col_inv)
                w = w - jnp.where(jnp.concatenate([mate, mate], axis=1) == ids, 2.0, 0.0)
                w = w.astype(jnp.bfloat16)
                weights[rows, cols] = w
                inner = w.astype(jnp.float32) * scores[rows, cols]
                inner = inner[:, :128] + inner[:, 128:]
                if chunk == 0:
                    sum_acc[rows, :] = inner
                else:
                    sum_acc[rows, :] += inner
                return carry

            lax.fori_loop(0, HALF // 64, weigh, 0)

        def coefs(j, carry):
            rows = pl.ds(pl.multiple_of(first + j * 64, 64), 64)
            r = rinv[rows, :]
            inner = jnp.sum(sum_acc[rows, :], axis=1, keepdims=True)
            pos_acc[rows, :] = r * r * inner
            sum_acc[rows, :] = r * temper
            return carry

        lax.fori_loop(0, HALF // 64, coefs, 0)

    def grad_piece(ahead, first):
        cols = pl.ds(pl.multiple_of(lax.rem(x + ahead, 4) * QUART, QUART), QUART)
        rows = pl.ds(first, HALF)
        d = jnp.dot(weights[rows, :], keys[:, cols], preferred_element_type=jnp.float32)
        u = sum_acc[rows, :]
        v = pos_acc[rows, :]
        return d * jnp.concatenate([u] * 3, axis=1) - emb[rows, cols] * jnp.concatenate([v] * 3, axis=1)

    rs_list = []

    def rs_message(src, dst, target):
        i = len(rs_list)
        copy = pltpu.make_async_remote_copy(
            src_ref=src, dst_ref=dst, send_sem=rs_send.at[i], recv_sem=rs_recv.at[i],
            device_id=target, device_id_type=MESH,
        )
        rs_list.append(copy)
        return copy

    far_right = rs_message(far_buf.at[0], relay_in.at[0], x_right)
    far_left = rs_message(far_buf.at[1], relay_in.at[1], x_left)
    right_bot = rs_message(near_buf.at[0], side_in.at[0], x_right)
    left_top = rs_message(near_buf.at[1], side_in.at[1], x_left)
    right_top = rs_message(near_buf.at[2], side_in.at[2], x_right)
    left_bot = rs_message(near_buf.at[3], side_in.at[3], x_left)
    cross = rs_message(cross_out, cross_in, dev_cross)
    y_first = [rs_message(yo_buf.at[a], yi_buf.at[a], dev_cross) for a in range(4)]
    x_second = {a: rs_message(xo_buf.at[a], xi_buf.at[a], {1: x_right, 2: x_far, 3: x_left}[a]) for a in (1, 2, 3)}

    lane_high = lane >= 64
    mine = lane_high == (yhi == 1)
    other = lane_high == (yhi == 0)
    f32, bf16 = jnp.float32, jnp.bfloat16

    def my_full(t0, t2):
        return jnp.where(yhi == 0, t0, t2)

    def send_y(a):
        d = grad_piece(a, HALF)
        t0, t1, t2 = d[:, :128], d[:, 128:256], d[:, 256:]
        yo_buf[a, 0:HALF, :] = my_full(t2, t0).astype(bf16)
        yo_buf[a, HALF:, :] = pack(t1, other).astype(bf16)
        y_first[a].start()
        hold_full[a] = my_full(t0, t2)
        hold_half[a] = t1

    def add_y(a):
        y_first[a].wait_recv()
        full = hold_full[a] + yi_buf[a, 0:HALF, :].astype(f32)
        half = hold_half[a] + unpack(yi_buf[a, HALF:, :].astype(f32))
        return full, half

    def send_x(a):
        full, half = add_y(a)
        xo_buf[a, 0:HALF, :] = full.astype(bf16)
        xo_buf[a, HALF:, :] = pack(half, mine).astype(bf16)
        x_second[a].start()

    weigh_rows(HALF)
    send_y(2)
    weigh_rows(0)
    d = grad_piece(2, 0)
    far_buf[0] = d[:FORTH].astype(bf16)
    far_right.start()
    far_buf[1] = d[FORTH:].astype(bf16)
    far_left.start()
    send_y(1)
    d = grad_piece(1, 0)
    near_buf[0] = d[FORTH:].astype(bf16)
    right_bot.start()
    hold_x[0] = d[:FORTH]
    d = grad_piece(3, 0)
    near_buf[1] = d[:FORTH].astype(bf16)
    left_top.start()
    hold_x[1] = d[FORTH:]
    send_y(3)
    send_y(0)
    send_x(2)
    far_right.wait_recv()
    near_buf[2] = (hold_x[0] + relay_in[0].astype(f32)).astype(bf16)
    right_top.start()
    far_left.wait_recv()
    near_buf[3] = (hold_x[1] + relay_in[1].astype(f32)).astype(bf16)
    left_bot.start()
    acc[...] = grad_piece(0, 0)
    right_bot.wait_recv()
    left_top.wait_recv()
    acc[FORTH:, :] += side_in[0].astype(f32)
    acc[:FORTH, :] += side_in[1].astype(f32)
    send_x(1)
    send_x(3)
    right_top.wait_recv()
    left_bot.wait_recv()
    acc[:FORTH, :] += side_in[2].astype(f32)
    acc[FORTH:, :] += side_in[3].astype(f32)
    t0, t1, t2 = acc[:, :128], acc[:, 128:256], acc[:, 256:]
    cross_out[0:HALF, :] = my_full(t2, t0).astype(bf16)
    cross_out[HALF:, :] = pack(t1, other).astype(bf16)
    cross.start()

    def write(first, full, half):
        rows = slice(first, first + HALF)
        full_turned = turn(full)
        grad_ref[rows, :128] = jnp.where(yhi == 0, full, jnp.where(lane_high, full_turned, turn(half)))
        grad_ref[rows, 128:] = jnp.where(yhi == 0, half, full_turned)[:, :64]

    full, half = add_y(0)
    for a in (2, 1, 3):
        x_second[a].wait_recv()
        full = full + xi_buf[a, 0:HALF, :].astype(f32)
        half = half + unpack(xi_buf[a, HALF:, :].astype(f32))
    write(HALF, full, half)
    cross.wait_recv()
    full = my_full(acc[:, :128], acc[:, 256:]) + cross_in[0:HALF, :].astype(f32)
    half = acc[:, 128:256] + unpack(cross_in[HALF:, :].astype(f32))
    write(0, full, half)
    near_all.wait_send()
    far_all.wait_send()
    stat_all.wait_send()
    for copy in rs_list:
        copy.wait_send()


def shards(embeddings, partner, inv_temp):
    f32, bf16 = jnp.float32, jnp.bfloat16
    vmem = pl.BlockSpec(memory_space=pltpu.VMEM)
    unit = HALF + FORTH
    loss, grad = pl.pallas_call(
        kernel,
        out_shape=(jax.ShapeDtypeStruct((1, ROWS), f32), jax.ShapeDtypeStruct((ROWS, 192), f32)),
        in_specs=[pl.BlockSpec(memory_space=pltpu.SMEM), vmem, pl.BlockSpec(memory_space=pl.ANY)],
        out_specs=(vmem, vmem),
        scratch_shapes=[
            pltpu.VMEM((ROWS, FEATS), f32),
            pltpu.VMEM((ROWS, FEATS), bf16),
            pltpu.VMEM((ROWS, 128), f32),
            pltpu.VMEM((KEYS, FEATS), bf16),
            pltpu.VMEM((ROWS, KEYS), f32),
            pltpu.VMEM((ROWS, KEYS), f32),
            pltpu.VMEM((ROWS, KEYS), bf16),
            pltpu.VMEM((ROWS, 128), f32),
            pltpu.VMEM((ROWS, 128), f32),
            pltpu.VMEM((ROWS, 128), f32),
            pltpu.VMEM((ROWS, 128), f32),
            pltpu.VMEM((2, ROWS), f32),
            pltpu.VMEM((8, 2, ROWS), f32),
            pltpu.VMEM((16, 128), f32),
            pltpu.VMEM((5, 16, 128), f32),
            pltpu.VMEM((16, 128), f32),
            pltpu.VMEM((8, 16, 128), f32),
            pltpu.VMEM((16, 128), f32),
            pltpu.VMEM((2, FORTH, QUART), bf16),
            pltpu.VMEM((4, FORTH, QUART), bf16),
            pltpu.VMEM((2, FORTH, QUART), bf16),
            pltpu.VMEM((4, FORTH, QUART), bf16),
            pltpu.VMEM((2, FORTH, QUART), f32),
            pltpu.VMEM((HALF, QUART), f32),
            pltpu.VMEM((4, HALF, 128), f32),
            pltpu.VMEM((4, HALF, 128), f32),
            pltpu.VMEM((4, unit, 128), bf16),
            pltpu.VMEM((4, unit, 128), bf16),
            pltpu.VMEM((unit, 128), bf16),
            pltpu.VMEM((unit, 128), bf16),
            pltpu.VMEM((4, unit, 128), bf16),
            pltpu.VMEM((4, unit, 128), bf16),
            pltpu.SemaphoreType.DMA((4,)),
            pltpu.SemaphoreType.DMA((76,)),
            pltpu.SemaphoreType.DMA((76,)),
            pltpu.SemaphoreType.DMA((2,)),
            pltpu.SemaphoreType.DMA((4,)),
            pltpu.SemaphoreType.DMA((14,)),
            pltpu.SemaphoreType.DMA((14,)),
        ],
        compiler_params=pltpu.CompilerParams(
            collective_id=0, has_side_effects=True, vmem_limit_bytes=61 * 1024 * 1024
        ),
    )(inv_temp, partner.reshape(1, ROWS), embeddings)
    return (loss.reshape(ROWS), grad)


def solution(mesh):
    in_specs = (P("blk", None), P("blk"), P())
    out_specs = (P("blk"), P("blk", "grp"))
    return jax.shard_map(shards, mesh=mesh, in_specs=in_specs, out_specs=out_specs, check_vma=False)
```

time: 343 us -> 72.6 us (0.21)
  waiting for transfers between devices: 215 us -> 0 us
  blocking collectives: 77.6 us -> 0 us
  Pallas kernels: 0 us -> 67.4 us
  matrix products: 18.9 us -> 0 us
  between operations: 15.4 us -> 1.28 us
  other arithmetic: 9.35 us -> 0 us
    psum x1 -> x0, waiting for transfers between devices: 142 us -> none  [shards(): full_grad = lax.psum(scaled, 'grp')]
    all_gather x1 -> x0, waiting for transfers between devices: 72.6 us -> none  [shards(): lax.all_gather(own_keys, 'blk', axis=0, tiled=True)]
    pallas_call x0 -> x1, Pallas kernels: none -> 67.4 us  [shards(): pl.pallas_call(kernel, out_shape=(jax.ShapeDtypeStruct((1, ROWS), f32), j...]
    unnamed x1 -> x0, blocking collectives: 57.3 us -> none
    psum x1 -> x0, blocking collectives: 20.3 us -> none  [shards(): lax.psum((jnp.sum(expon, axis=1), jnp.sum(jnp.where(is_mate, scores, 0.0)...]
    dot_general x2 -> x0, matrix products: 18.9 us -> none  [the longest x1 9.8 us: shards(): jnp.dot(weights.astype(jnp.bfloat16), key_piece, preferred_element_type=j...]
    reduce_sum x2 -> x0, other arithmetic: 4.8 us -> none  [the longest x1 2.48 us: shards(): inner = jnp.sum(unit * full_grad, axis=1, keepdims=True)]
  transfers between devices with their start and end apart: 2 -> 0, of which waited for: 2 -> 0; matrix products, arithmetic and copies ran while one was open for 0% -> 0% of each run, Pallas kernels for 0% -> 0%
where the time goes in v2:
time: 72.6 us; the launch traced here: 71.9 us
  Pallas kernels  67.4 us (93%)
  local copies, waits for them, and re-layouts  3.22 us (4%)
  between operations  1.28 us (2%)
    pallas_call x1, Pallas kernels, shards(): pl.pallas_call(kernel, out_shape=(jax.ShapeDtypeStruct((1, ROWS), f32), j...  67.4 us
    unnamed x2, local copies, waits for them, and re-layouts  3.22 us

profile of v2, /device:TPU:1, one launch (start us, length us, event | category | flops | bytes accessed | tf_op | source)
XLA Modules:
  0.0 71.9 jit_solution(2029233949618912090)
XLA Ops:
  1.3 67.4 %shard_map.50 = (f32[1,512]{1,0:T(1,128)}, f32[512,192]{1,0:T(8,128)}) custom-call(s32[1]{0:T(128)S(6)} %copy.7.temp_ref, s32[1,512]{1,0:T(1,128)} %bitcast.2, f32[512,1536]{1,0:T(8,128)} %emb_hbm.1), custom_call_target="tpu_custom_call" | custom-call | tf_op jit(solution)/shard_map/pallas_call | solution.py:488
  68.7 2.0 %copy.5 = f32[512,192]{0,1:T(8,128)} copy(f32[512,192]{1,0:T(8,128)} %get-tuple-element.7) | data formatting | bytes 786432
  70.6 1.3 %copy.8 = f32[512]{0:T(512)} copy(f32[512]{0:T(512)} %bitcast.3) | data formatting | bytes 4096

commit v3 on v2

--- a/solution.py
+++ b/solution.py
@@ -14,6 +14,7 @@
 QUART = 384
 HALF = 256
 FORTH = 128
+ORDER = (0, 2, 1, 3)
 
 
 def tile_of(dist, side, other_y):
@@ -139,7 +140,7 @@
 
     ring, across, twin = {}, {}, {}
     for dist in range(1, 5):
-        for piece in range(4):
+        for piece in ORDER:
             for side in (0, 1):
                 if dist == 4 and side != piece // 2:
                     continue
@@ -175,38 +176,39 @@
             ids.append((((yk * 8 + zk) * 2 + ck) * ROWS + x * 128 + within).astype(jnp.float32))
         return jnp.concatenate(ids, axis=1)
 
-    def score_chunk(chunk):
+    def score_half(chunk, half):
         cols = slice(chunk * CHUNK, (chunk + 1) * CHUNK)
+        rows = slice(half * HALF, (half + 1) * HALF)
         ids = key_ids(chunk)
-
-        def step(j, carry):
-            rows = pl.ds(pl.multiple_of(j * HALF, HALF), HALF)
-            s = temper * lax.dot_general(
-                query[rows, :], keys[cols, :], (((1,), (1,)), ((), ())), preferred_element_type=jnp.float32
-            )
-            e = jnp.exp(s - temper)
-            if chunk == 0:
-                own = lax.broadcasted_iota(jnp.int32, (HALF, CHUNK), 0) + (blk * ROWS + j * HALF)
-                e = jnp.where(own.astype(jnp.float32) == ids, 0.0, e)
-            mate = mate_col[rows, :]
-            mate = jnp.concatenate([mate, mate], axis=1)
-            p = jnp.where(mate == ids, s, 0.0)
-            scores[rows, cols] = s
-            expon[rows, cols] = e
-            if chunk == 0:
-                sum_acc[rows, :] = e[:, :128] + e[:, 128:]
-                pos_acc[rows, :] = p[:, :128] + p[:, 128:]
-            else:
-                sum_acc[rows, :] += e[:, :128] + e[:, 128:]
-                pos_acc[rows, :] += p[:, :128] + p[:, 128:]
-            return carry + jnp.sum(e, axis=0, keepdims=True)
-
-        total = lax.fori_loop(0, ROWS // HALF, step, jnp.zeros((1, CHUNK), jnp.float32))
+        s = temper * lax.dot_general(
+            query[rows, :], keys[cols, :], (((1,), (1,)), ((), ())), preferred_element_type=jnp.float32
+        )
+        e = jnp.exp(s - temper)
+        if chunk == 0:
+            own = lax.broadcasted_iota(jnp.int32, (HALF, CHUNK), 0) + (blk * ROWS + half * HALF)
+            e = jnp.where(own.astype(jnp.float32) == ids, 0.0, e)
+        mate = mate_col[rows, :]
+        mate = jnp.concatenate([mate, mate], axis=1)
+        p = jnp.where(mate == ids, s, 0.0)
+        scores[rows, cols] = s
+        expon[rows, cols] = e
+        if chunk == 0:
+            sum_acc[rows, :] = e[:, :128] + e[:, 128:]
+            pos_acc[rows, :] = p[:, :128] + p[:, 128:]
+        else:
+            sum_acc[rows, :] += e[:, :128] + e[:, 128:]
+            pos_acc[rows, :] += p[:, :128] + p[:, 128:]
+        total = jnp.sum(e, axis=0, keepdims=True)
         for i in (0, 1):
             zk, other = tile_place(2 * chunk + i)
-            col_out[pl.ds(other * 8 + zk, 1), :] = total[:, 128 * i : 128 * (i + 1)]
-
-    for piece in range(4):
+            row = pl.ds(other * 8 + zk, 1)
+            part = total[:, 128 * i : 128 * (i + 1)]
+            if half == 0:
+                col_out[row, :] = part
+            else:
+                col_out[row, :] += part
+
+    for piece in ORDER:
         for side in (0, 1):
             ring[side, 1, piece].start()
         across[0, 0, piece].start()
@@ -220,7 +222,7 @@
 
     def finish_across(dist):
         for side in sides(dist):
-            for piece in range(4):
+            for piece in ORDER:
                 across[side, dist, piece].wait_recv()
             twin[side, dist, 1].start()
 
@@ -228,52 +230,61 @@
         for side in sides(dist):
             twin[side, dist, other].wait_recv()
 
+    def meanwhile(dist, turn_):
+        if dist == 1:
+            if turn_ == 0:
+                loads[2].wait()
+                normalize(2)
+            elif turn_ == 1:
+                loads[3].wait()
+                normalize(3)
+                mate_row = jnp.broadcast_to(partner_ref[...].astype(jnp.float32), (128, ROWS))
+                mate_col[...] = mate_row.T
+            elif turn_ == 2:
+                finish_across(0)
+            else:
+                finish_twin(0, 0)
+                finish_twin(0, 1)
+                score_half(0, 0)
+        elif turn_ == 0:
+            score_half(2 * (dist - 2), 1)
+        elif turn_ == 1:
+            finish_twin(dist - 1, 0)
+            score_half(2 * (dist - 1) - 1, 0)
+        elif turn_ == 2:
+            score_half(2 * (dist - 1) - 1, 1)
+            finish_across(dist - 1)
+        else:
+            finish_twin(dist - 1, 1)
+            score_half(2 * (dist - 1), 0)
+
     for dist in range(1, 4):
-        for piece in range(4):
+        for turn_, piece in enumerate(ORDER):
             for side in (0, 1):
                 ring[side, dist, piece].wait_recv()
                 if dist < 3 or side == piece // 2:
                     ring[side, dist + 1, piece].start()
                 across[side, dist, piece].start()
-                if piece == 3:
+                if turn_ == 3:
                     twin[side, dist, 0].start()
-            if dist == 1:
-                if piece == 0:
-                    loads[2].wait()
-                    normalize(2)
-                elif piece == 1:
-                    loads[3].wait()
-                    normalize(3)
-                    mate_row = jnp.broadcast_to(partner_ref[...].astype(jnp.float32), (128, ROWS))
-                    mate_col[...] = mate_row.T
-                elif piece == 2:
-                    finish_across(0)
-                else:
-                    finish_twin(0, 0)
-                    finish_twin(0, 1)
-                    score_chunk(0)
-            else:
-                if piece == 0:
-                    finish_twin(dist - 1, 0)
-                    score_chunk(2 * (dist - 1) - 1)
-                elif piece == 1:
-                    finish_across(dist - 1)
-                elif piece == 2:
-                    finish_twin(dist - 1, 1)
-                    score_chunk(2 * (dist - 1))
-    for piece in (0, 2, 1, 3):
+            meanwhile(dist, turn_)
+    for piece in (0, 2):
+        ring[piece // 2, 4, piece].wait_recv()
+        across[0, 4, piece].start()
+    meanwhile(4, 0)
+    for piece in (1, 3):
         ring[piece // 2, 4, piece].wait_recv()
         across[0, 4, piece].start()
     twin[0, 4, 0].start()
-    finish_twin(3, 0)
-    score_chunk(5)
-    finish_across(3)
-    finish_twin(3, 1)
-    score_chunk(6)
+    meanwhile(4, 1)
+    meanwhile(4, 2)
+    meanwhile(4, 3)
+    score_half(6, 1)
     finish_across(4)
     finish_twin(4, 0)
     finish_twin(4, 1)
-    score_chunk(7)
+    score_half(7, 0)
+    score_half(7, 1)
 
     def small(src, dst, sems, i, target):
         return pltpu.make_async_remote_copy(
@@ -488,7 +499,7 @@
     loss, grad = pl.pallas_call(
         kernel,
         out_shape=(jax.ShapeDtypeStruct((1, ROWS), f32), jax.ShapeDtypeStruct((ROWS, 192), f32)),
-        in_specs=[pl.BlockSpec(memory_space=pltpu.SMEM), vmem, pl.BlockSpec(memory_space=pl.ANY)],
+        in_specs=[pl.BlockSpec(memory_space=pltpu.SMEM), vmem, pl.BlockSpec(memory_space=pltpu.HBM)],
         out_specs=(vmem, vmem),
         scratch_shapes=[
             pltpu.VMEM((ROWS, FEATS), f32),
@@ -532,7 +543,7 @@
             pltpu.SemaphoreType.DMA((14,)),
         ],
         compiler_params=pltpu.CompilerParams(
-            collective_id=0, has_side_effects=True, vmem_limit_bytes=61 * 1024 * 1024
+            collective_id=0, has_side_effects=True, vmem_limit_bytes=53 * 1024 * 1024
         ),
     )(inv_temp, partner.reshape(1, ROWS), embeddings)
     return (loss.reshape(ROWS), grad)

time: 72.6 us -> 65.5 us (0.902)
  Pallas kernels: 67.4 us -> 61.4 us
  local copies, waits for them, and re-layouts: 3.22 us -> 2.18 us
    pallas_call x1, Pallas kernels: 67.4 us -> 61.4 us  [shards(): pl.pallas_call(kernel, out_shape=(jax.ShapeDtypeStruct((1, ROWS), f32), j...]
    unnamed x2 -> x4, local copies, waits for them, and re-layouts: 3.22 us -> 2.18 us
where the time goes in v3:
time: 65.5 us; the launch traced here: 64.9 us
  Pallas kernels  61.4 us (94%)
  local copies, waits for them, and re-layouts  2.18 us (3%)
  between operations  1.29 us (2%)
    pallas_call x1, Pallas kernels, shards(): pl.pallas_call(kernel, out_shape=(jax.ShapeDtypeStruct((1, ROWS), f32), j...  61.4 us
    unnamed x4, local copies, waits for them, and re-layouts  2.18 us

profile of v3, /device:TPU:1, one launch (start us, length us, event | category | flops | bytes accessed | tf_op | source)
XLA Modules:
  0.0 64.9 jit_solution(14841598967198872104)
XLA Ops:
  1.3 0.0 copy-start
  1.3 0.7 %copy-done = s32[512]{0:T(512)S(1)} copy-done((s32[512]{0:T(512)S(1)}, s32[512]{0:T(512)}, u32[]{:S(2)}) %copy-start) | copy-done | bytes 2072
  2.0 61.4 %shard_map.50 = (f32[1,512]{1,0:T(1,128)S(1)}, f32[512,192]{1,0:T(8,128)S(1)}) custom-call(s32[1]{0:T(128)S(6)} %copy.7.temp_ref, s32[1,512]{1,0:T(1,128)S(1)} %bitcast.2, f32[512,1536]{1,0:T(8,128)} %emb_hbm.1), custom_call_target="tpu_custom_call" | custom-call | tf_op jit(solution)/shard_map/pallas_call | solution.py:499
  63.4 0.9 %copy.5 = f32[512,192]{0,1:T(8,128)} copy(f32[512,192]{1,0:T(8,128)S(1)} %get-tuple-element.7) | data formatting | bytes 786432
  64.3 0.6 copy.8
Async XLA Ops:
  1.3 0.7 %copy-start = (s32[512]{0:T(512)S(1)}, s32[512]{0:T(512)}, u32[]{:S(2)}) copy-start(s32[512]{0:T(512)} %param.4) | copy-start | bytes 6148

commit v4 on v3

--- a/solution.py
+++ b/solution.py
@@ -293,7 +293,7 @@
         )
 
     near_targets = [sib, dev_a, dev_b, device(x, y_a, z, 1 - core), device(x, y_b, z, 1 - core)]
-    for i, target in enumerate(near_targets):
+    for i, target in reversed(list(enumerate(near_targets))):
         small(col_out, col_near.at[i], col_sem, 0, target).start()
     stat_out[0:1, :] = jnp.sum(sum_acc[...].T, axis=0, keepdims=True)
     stat_out[1:2, :] = jnp.sum(pos_acc[...].T, axis=0, keepdims=True)
@@ -311,8 +311,6 @@
     col_sum[...] = col_out[...] + turn(col_near[0]) + jnp.where(is_a, over_a, over_b)
     for dz in range(1, 8):
         small(col_sum, col_far.at[dz], col_sem, 2, device(x, y, lax.rem(z + dz, 8), core)).start()
-    for copy in messages:
-        copy.wait_send()
     stat_all = small(stat_in.at[pl.ds(1, 7)], stat_in.at[pl.ds(1, 7)], stat_sem, 0, peers[0])
     stat_all.wait_recv()
     total = stat_out[...]
@@ -357,7 +355,7 @@
                     sum_acc[rows, :] += inner
                 return carry
 
-            lax.fori_loop(0, HALF // 64, weigh, 0)
+            lax.fori_loop(0, FORTH // 64, weigh, 0)
 
         def coefs(j, carry):
             rows = pl.ds(pl.multiple_of(first + j * 64, 64), 64)
@@ -367,11 +365,11 @@
             sum_acc[rows, :] = r * temper
             return carry
 
-        lax.fori_loop(0, HALF // 64, coefs, 0)
+        lax.fori_loop(0, FORTH // 64, coefs, 0)
 
     def grad_piece(ahead, first):
         cols = pl.ds(pl.multiple_of(lax.rem(x + ahead, 4) * QUART, QUART), QUART)
-        rows = pl.ds(first, HALF)
+        rows = pl.ds(first, FORTH)
         d = jnp.dot(weights[rows, :], keys[:, cols], preferred_element_type=jnp.float32)
         u = sum_acc[rows, :]
         v = pos_acc[rows, :]
@@ -388,16 +386,6 @@
         rs_list.append(copy)
         return copy
 
-    far_right = rs_message(far_buf.at[0], relay_in.at[0], x_right)
-    far_left = rs_message(far_buf.at[1], relay_in.at[1], x_left)
-    right_bot = rs_message(near_buf.at[0], side_in.at[0], x_right)
-    left_top = rs_message(near_buf.at[1], side_in.at[1], x_left)
-    right_top = rs_message(near_buf.at[2], side_in.at[2], x_right)
-    left_bot = rs_message(near_buf.at[3], side_in.at[3], x_left)
-    cross = rs_message(cross_out, cross_in, dev_cross)
-    y_first = [rs_message(yo_buf.at[a], yi_buf.at[a], dev_cross) for a in range(4)]
-    x_second = {a: rs_message(xo_buf.at[a], xi_buf.at[a], {1: x_right, 2: x_far, 3: x_left}[a]) for a in (1, 2, 3)}
-
     lane_high = lane >= 64
     mine = lane_high == (yhi == 1)
     other = lane_high == (yhi == 0)
@@ -406,99 +394,150 @@
     def my_full(t0, t2):
         return jnp.where(yhi == 0, t0, t2)
 
-    def send_y(a):
-        d = grad_piece(a, HALF)
+    def write(first, full, half):
+        rows = slice(first, first + FORTH)
+        full, half = full.T, half.T
+        grad_ref[0:64, rows] = jnp.where(yhi == 0, full[:64], half[64:])
+        grad_ref[64:128, rows] = jnp.where(yhi == 0, full[64:], full[:64])
+        grad_ref[128:192, rows] = jnp.where(yhi == 0, half[:64], full[64:])
+
+    top, bot = slice(0, FORTH // 2), slice(FORTH // 2, FORTH)
+    far_right, far_left, right_bot, left_top, right_top, left_bot, cross = ([] for _ in range(7))
+    for q in (0, 1):
+        far_right.append(rs_message(far_buf.at[q, 0], relay_in.at[q, 0], x_right))
+        far_left.append(rs_message(far_buf.at[q, 1], relay_in.at[q, 1], x_left))
+        right_bot.append(rs_message(near_buf.at[q, 0], side_in.at[q, 0], x_right))
+        left_top.append(rs_message(near_buf.at[q, 1], side_in.at[q, 1], x_left))
+        right_top.append(rs_message(near_buf.at[q, 2], side_in.at[q, 2], x_right))
+        left_bot.append(rs_message(near_buf.at[q, 3], side_in.at[q, 3], x_left))
+        cross.append(rs_message(cross_out.at[q], cross_in.at[q], dev_cross))
+
+    def x_far_parts(q):
+        d = grad_piece(2, FORTH * q)
+        far_buf[q, 0] = d[top].astype(bf16)
+        far_right[q].start()
+        far_buf[q, 1] = d[bot].astype(bf16)
+        far_left[q].start()
+
+    def x_near_parts(q):
+        d = grad_piece(1, FORTH * q)
+        near_buf[q, 0] = d[bot].astype(bf16)
+        right_bot[q].start()
+        hold_x[q, 0] = d[top]
+        d = grad_piece(3, FORTH * q)
+        near_buf[q, 1] = d[top].astype(bf16)
+        left_top[q].start()
+        hold_x[q, 1] = d[bot]
+
+    def x_relay(q):
+        far_right[q].wait_recv()
+        near_buf[q, 2] = (hold_x[q, 0] + relay_in[q, 0].astype(f32)).astype(bf16)
+        right_top[q].start()
+        far_left[q].wait_recv()
+        near_buf[q, 3] = (hold_x[q, 1] + relay_in[q, 1].astype(f32)).astype(bf16)
+        left_bot[q].start()
+
+    def x_own(q):
+        acc[q] = grad_piece(0, FORTH * q)
+
+    def x_sum(q):
+        for copies in (right_bot, left_top, right_top, left_bot):
+            copies[q].wait_recv()
+        high = acc[q, top, :] + side_in[q, 1].astype(f32) + side_in[q, 2].astype(f32)
+        low = acc[q, bot, :] + side_in[q, 0].astype(f32) + side_in[q, 3].astype(f32)
+        d = jnp.concatenate([high, low], axis=0)
         t0, t1, t2 = d[:, :128], d[:, 128:256], d[:, 256:]
-        yo_buf[a, 0:HALF, :] = my_full(t2, t0).astype(bf16)
-        yo_buf[a, HALF:, :] = pack(t1, other).astype(bf16)
-        y_first[a].start()
-        hold_full[a] = my_full(t0, t2)
-        hold_half[a] = t1
-
-    def add_y(a):
-        y_first[a].wait_recv()
-        full = hold_full[a] + yi_buf[a, 0:HALF, :].astype(f32)
-        half = hold_half[a] + unpack(yi_buf[a, HALF:, :].astype(f32))
+        cross_out[q, 0:FORTH, :] = my_full(t2, t0).astype(bf16)
+        cross_out[q, FORTH:, :] = pack(t1, other).astype(bf16)
+        cross[q].start()
+        acc[q, :, 0:128] = my_full(t0, t2)
+        acc[q, :, 128:256] = t1
+
+    def x_finish(q):
+        cross[q].wait_recv()
+        full = acc[q, :, 0:128] + cross_in[q, 0:FORTH, :].astype(f32)
+        half = acc[q, :, 128:256] + unpack(cross_in[q, FORTH:, :].astype(f32))
+        write(FORTH * q, full, half)
+
+    y_first = [[rs_message(yo_buf.at[q, a], yi_buf.at[q, a], dev_cross) for a in range(4)] for q in (0, 1)]
+    to = {1: x_right, 2: x_far, 3: x_left}
+    x_second = [{a: rs_message(xo_buf.at[q, a], xi_buf.at[q, a], to[a]) for a in (1, 2, 3)} for q in (0, 1)]
+
+    def y_send(q, a):
+        d = grad_piece(a, HALF + FORTH * q)
+        t0, t1, t2 = d[:, :128], d[:, 128:256], d[:, 256:]
+        yo_buf[q, a, 0:FORTH, :] = my_full(t2, t0).astype(bf16)
+        yo_buf[q, a, FORTH:, :] = pack(t1, other).astype(bf16)
+        y_first[q][a].start()
+        hold_full[q, a] = my_full(t0, t2)
+        hold_half[q, a] = t1
+
+    def y_add(q, a):
+        y_first[q][a].wait_recv()
+        full = hold_full[q, a] + yi_buf[q, a, 0:FORTH, :].astype(f32)
+        half = hold_half[q, a] + unpack(yi_buf[q, a, FORTH:, :].astype(f32))
         return full, half
 
-    def send_x(a):
-        full, half = add_y(a)
-        xo_buf[a, 0:HALF, :] = full.astype(bf16)
-        xo_buf[a, HALF:, :] = pack(half, mine).astype(bf16)
-        x_second[a].start()
-
+    def y_then_x(q, a):
+        full, half = y_add(q, a)
+        xo_buf[q, a, 0:FORTH, :] = full.astype(bf16)
+        xo_buf[q, a, FORTH:, :] = pack(half, mine).astype(bf16)
+        x_second[q][a].start()
+
+    def y_finish(q):
+        full, half = y_add(q, 0)
+        for a in (2, 1, 3):
+            x_second[q][a].wait_recv()
+            full = full + xi_buf[q, a, 0:FORTH, :].astype(f32)
+            half = half + unpack(xi_buf[q, a, FORTH:, :].astype(f32))
+        write(HALF + FORTH * q, full, half)
+
+    weigh_rows(0)
+    x_far_parts(0)
     weigh_rows(HALF)
-    send_y(2)
-    weigh_rows(0)
-    d = grad_piece(2, 0)
-    far_buf[0] = d[:FORTH].astype(bf16)
-    far_right.start()
-    far_buf[1] = d[FORTH:].astype(bf16)
-    far_left.start()
-    send_y(1)
-    d = grad_piece(1, 0)
-    near_buf[0] = d[FORTH:].astype(bf16)
-    right_bot.start()
-    hold_x[0] = d[:FORTH]
-    d = grad_piece(3, 0)
-    near_buf[1] = d[:FORTH].astype(bf16)
-    left_top.start()
-    hold_x[1] = d[FORTH:]
-    send_y(3)
-    send_y(0)
-    send_x(2)
-    far_right.wait_recv()
-    near_buf[2] = (hold_x[0] + relay_in[0].astype(f32)).astype(bf16)
-    right_top.start()
-    far_left.wait_recv()
-    near_buf[3] = (hold_x[1] + relay_in[1].astype(f32)).astype(bf16)
-    left_bot.start()
-    acc[...] = grad_piece(0, 0)
-    right_bot.wait_recv()
-    left_top.wait_recv()
-    acc[FORTH:, :] += side_in[0].astype(f32)
-    acc[:FORTH, :] += side_in[1].astype(f32)
-    send_x(1)
-    send_x(3)
-    right_top.wait_recv()
-    left_bot.wait_recv()
-    acc[:FORTH, :] += side_in[2].astype(f32)
-    acc[FORTH:, :] += side_in[3].astype(f32)
-    t0, t1, t2 = acc[:, :128], acc[:, 128:256], acc[:, 256:]
-    cross_out[0:HALF, :] = my_full(t2, t0).astype(bf16)
-    cross_out[HALF:, :] = pack(t1, other).astype(bf16)
-    cross.start()
-
-    def write(first, full, half):
-        rows = slice(first, first + HALF)
-        full_turned = turn(full)
-        grad_ref[rows, :128] = jnp.where(yhi == 0, full, jnp.where(lane_high, full_turned, turn(half)))
-        grad_ref[rows, 128:] = jnp.where(yhi == 0, half, full_turned)[:, :64]
-
-    full, half = add_y(0)
-    for a in (2, 1, 3):
-        x_second[a].wait_recv()
-        full = full + xi_buf[a, 0:HALF, :].astype(f32)
-        half = half + unpack(xi_buf[a, HALF:, :].astype(f32))
-    write(HALF, full, half)
-    cross.wait_recv()
-    full = my_full(acc[:, :128], acc[:, 256:]) + cross_in[0:HALF, :].astype(f32)
-    half = acc[:, 128:256] + unpack(cross_in[HALF:, :].astype(f32))
-    write(0, full, half)
+    y_send(0, 2)
+    y_send(0, 1)
+    weigh_rows(FORTH)
+    x_far_parts(1)
+    x_near_parts(0)
+    y_send(0, 3)
+    x_relay(0)
+    weigh_rows(HALF + FORTH)
+    y_send(1, 2)
+    x_near_parts(1)
+    x_relay(1)
+    y_send(1, 1)
+    y_send(1, 3)
+    y_send(0, 0)
+    y_send(1, 0)
+    x_own(0)
+    x_sum(0)
+    y_then_x(0, 2)
+    x_own(1)
+    x_sum(1)
+    y_then_x(0, 1)
+    y_then_x(0, 3)
+    y_then_x(1, 2)
+    y_then_x(1, 1)
+    y_then_x(1, 3)
+    y_finish(0)
+    x_finish(0)
+    y_finish(1)
+    x_finish(1)
     near_all.wait_send()
     far_all.wait_send()
     stat_all.wait_send()
-    for copy in rs_list:
+    for copy in messages + rs_list:
         copy.wait_send()
 
 
 def shards(embeddings, partner, inv_temp):
     f32, bf16 = jnp.float32, jnp.bfloat16
     vmem = pl.BlockSpec(memory_space=pltpu.VMEM)
-    unit = HALF + FORTH
+    unit = FORTH + FORTH // 2
     loss, grad = pl.pallas_call(
         kernel,
-        out_shape=(jax.ShapeDtypeStruct((1, ROWS), f32), jax.ShapeDtypeStruct((ROWS, 192), f32)),
+        out_shape=(jax.ShapeDtypeStruct((1, ROWS), f32), jax.ShapeDtypeStruct((192, ROWS), f32)),
         in_specs=[pl.BlockSpec(memory_space=pltpu.SMEM), vmem, pl.BlockSpec(memory_space=pltpu.HBM)],
         out_specs=(vmem, vmem),
         scratch_shapes=[
@@ -520,33 +559,33 @@
             pltpu.VMEM((16, 128), f32),
             pltpu.VMEM((8, 16, 128), f32),
             pltpu.VMEM((16, 128), f32),
-            pltpu.VMEM((2, FORTH, QUART), bf16),
-            pltpu.VMEM((4, FORTH, QUART), bf16),
-            pltpu.VMEM((2, FORTH, QUART), bf16),
-            pltpu.VMEM((4, FORTH, QUART), bf16),
+            pltpu.VMEM((2, 2, FORTH // 2, QUART), bf16),
+            pltpu.VMEM((2, 4, FORTH // 2, QUART), bf16),
+            pltpu.VMEM((2, 2, FORTH // 2, QUART), bf16),
+            pltpu.VMEM((2, 4, FORTH // 2, QUART), bf16),
+            pltpu.VMEM((2, 2, FORTH // 2, QUART), f32),
             pltpu.VMEM((2, FORTH, QUART), f32),
-            pltpu.VMEM((HALF, QUART), f32),
-            pltpu.VMEM((4, HALF, 128), f32),
-            pltpu.VMEM((4, HALF, 128), f32),
-            pltpu.VMEM((4, unit, 128), bf16),
-            pltpu.VMEM((4, unit, 128), bf16),
-            pltpu.VMEM((unit, 128), bf16),
-            pltpu.VMEM((unit, 128), bf16),
-            pltpu.VMEM((4, unit, 128), bf16),
-            pltpu.VMEM((4, unit, 128), bf16),
+            pltpu.VMEM((2, 4, FORTH, 128), f32),
+            pltpu.VMEM((2, 4, FORTH, 128), f32),
+            pltpu.VMEM((2, 4, unit, 128), bf16),
+            pltpu.VMEM((2, 4, unit, 128), bf16),
+            pltpu.VMEM((2, unit, 128), bf16),
+            pltpu.VMEM((2, unit, 128), bf16),
+            pltpu.VMEM((2, 4, unit, 128), bf16),
+            pltpu.VMEM((2, 4, unit, 128), bf16),
             pltpu.SemaphoreType.DMA((4,)),
             pltpu.SemaphoreType.DMA((76,)),
             pltpu.SemaphoreType.DMA((76,)),
             pltpu.SemaphoreType.DMA((2,)),
             pltpu.SemaphoreType.DMA((4,)),
-            pltpu.SemaphoreType.DMA((14,)),
-            pltpu.SemaphoreType.DMA((14,)),
+            pltpu.SemaphoreType.DMA((28,)),
+            pltpu.SemaphoreType.DMA((28,)),
         ],
         compiler_params=pltpu.CompilerParams(
             collective_id=0, has_side_effects=True, vmem_limit_bytes=53 * 1024 * 1024
         ),
     )(inv_temp, partner.reshape(1, ROWS), embeddings)
-    return (loss.reshape(ROWS), grad)
+    return (loss.reshape(ROWS), grad.T)
 
 
 def solution(mesh):

time: 65.5 us -> 63.7 us (0.973)
  Pallas kernels: 61.4 us -> 60.3 us
    pallas_call x1, Pallas kernels: 61.4 us -> 60.3 us  [shards(): pl.pallas_call(kernel, out_shape=(jax.ShapeDtypeStruct((1, ROWS), f32), j...]
where the time goes in v4:
time: 63.7 us; the launch traced here: 63.6 us
  Pallas kernels  60.3 us (95%)
  local copies, waits for them, and re-layouts  2 us (3%)
  between operations  1.29 us (2%)
    pallas_call x1, Pallas kernels, shards(): pl.pallas_call(kernel, out_shape=(jax.ShapeDtypeStruct((1, ROWS), f32), j...  60.3 us
    unnamed x4, local copies, waits for them, and re-layouts  2 us

profile of v4, /device:TPU:1, one launch (start us, length us, event | category | flops | bytes accessed | tf_op | source)
XLA Modules:
  0.0 63.6 jit_solution(11046626965703101391)
XLA Ops:
  1.3 0.0 copy-start
  1.3 0.7 %copy-done = s32[512]{0:T(512)S(1)} copy-done((s32[512]{0:T(512)S(1)}, s32[512]{0:T(512)}, u32[]{:S(2)}) %copy-start) | copy-done | bytes 2072
  2.0 60.3 %shard_map.50 = (f32[1,512]{1,0:T(1,128)S(1)}, f32[192,512]{1,0:T(8,128)S(1)}) custom-call(s32[1]{0:T(128)S(6)} %copy.7.temp_ref, s32[1,512]{1,0:T(1,128)S(1)} %bitcast.4, f32[512,1536]{1,0:T(8,128)} %emb_hbm.1), custom_call_target="tpu_custom_call" | custom-call | tf_op jit(solution)/shard_map/pallas_call | solution.py:538
  62.3 0.6 copy.8
  62.8 0.7 %copy.9 = f32[512,192]{0,1:T(8,128)} copy(f32[512,192]{0,1:T(8,128)S(1)} %bitcast.3) | data formatting | bytes 786432
Async XLA Ops:
  1.3 0.7 %copy-start = (s32[512]{0:T(512)S(1)}, s32[512]{0:T(512)}, u32[]{:S(2)}) copy-start(s32[512]{0:T(512)} %param.4) | copy-start | bytes 6148

commit v5 on v4

--- a/solution.py
+++ b/solution.py
@@ -54,7 +54,7 @@
     stat_out, stat_in, col_out, col_near, col_sum, col_far, key_tot,
     far_buf, near_buf, relay_in, side_in, hold_x, acc, hold_full, hold_half,
     yo_buf, yi_buf, cross_out, cross_in, xo_buf, xi_buf,
-    load_sem, ag_send, ag_recv, stat_sem, col_sem, rs_send, rs_recv,
+    load_sem, ag_send, ag_recv, stat_sem, col_sem, rs_recv,
 ):
     blk = lax.axis_index("blk")
     grp = lax.axis_index("grp")
@@ -123,42 +123,55 @@
 
     pl.semaphore_wait(barrier, len(greeted))
 
-    messages = []
-
-    def message(src, dst, rows, target):
-        i = len(messages)
-        copy = pltpu.make_async_remote_copy(
+    def message(src, dst, rows, target, send, recv):
+        return pltpu.make_async_remote_copy(
             src_ref=keys.at[pl.ds(src, rows)],
             dst_ref=keys.at[pl.ds(dst, rows)],
-            send_sem=ag_send.at[i],
-            recv_sem=ag_recv.at[i],
+            send_sem=ag_send.at[send],
+            recv_sem=ag_recv.at[recv],
             device_id=target,
             device_id_type=MESH,
         )
-        messages.append(copy)
-        return copy
 
     ring, across, twin = {}, {}, {}
+
+    def ring_sem(dist, turn_):
+        return 4 * (dist - 1) + turn_
+
     for dist in range(1, 5):
-        for piece in ORDER:
+        for turn_, piece in enumerate(ORDER):
             for side in (0, 1):
                 if dist == 4 and side != piece // 2:
                     continue
                 src = slot(dist - 1, 0 if dist == 1 else side, 0, 0, piece)
                 dst = slot(dist, 0 if dist == 4 else side, 0, 0, piece)
-                ring[side, dist, piece] = message(src, dst, SUB, z_right if side == 0 else z_left)
+                sem = ring_sem(dist, turn_ if dist < 4 else turn_ // 2)
+                ring[side, dist, piece] = message(src, dst, SUB, z_right if side == 0 else z_left, 0, sem)
     for dist in range(5):
         for side in (0, 1):
             if dist in (0, 4) and side == 1:
                 continue
             for piece in range(4):
                 across[side, dist, piece] = message(
-                    slot(dist, side, 0, 0, piece), slot(dist, side, 1, 0, piece), SUB, dev_a if piece < 2 else dev_b
+                    slot(dist, side, 0, 0, piece),
+                    slot(dist, side, 1, 0, piece),
+                    SUB,
+                    dev_a if piece < 2 else dev_b,
+                    0,
+                    14 + dist,
                 )
             for other in (0, 1):
                 twin[side, dist, other] = message(
-                    slot(dist, side, other, 0, 0), slot(dist, side, other, 1, 0), 4 * SUB, sib
+                    slot(dist, side, other, 0, 0),
+                    slot(dist, side, other, 1, 0),
+                    4 * SUB,
+                    sib,
+                    1,
+                    19 + 2 * dist + other,
                 )
+
+    def wait_ring(dist, turn_):
+        message(0, 0, 2 * SUB, sib, 0, ring_sem(dist, turn_)).wait_recv()
 
     lane = lax.broadcasted_iota(jnp.int32, (1, 128), 1)
 
@@ -221,14 +234,12 @@
         return (0,) if dist in (0, 4) else (0, 1)
 
     def finish_across(dist):
+        message(0, 0, 4 * SUB * len(sides(dist)), sib, 0, 14 + dist).wait_recv()
         for side in sides(dist):
-            for piece in ORDER:
-                across[side, dist, piece].wait_recv()
             twin[side, dist, 1].start()
 
     def finish_twin(dist, other):
-        for side in sides(dist):
-            twin[side, dist, other].wait_recv()
+        message(0, 0, 4 * SUB * len(sides(dist)), sib, 1, 19 + 2 * dist + other).wait_recv()
 
     def meanwhile(dist, turn_):
         if dist == 1:
@@ -260,20 +271,20 @@
 
     for dist in range(1, 4):
         for turn_, piece in enumerate(ORDER):
+            wait_ring(dist, turn_)
             for side in (0, 1):
-                ring[side, dist, piece].wait_recv()
                 if dist < 3 or side == piece // 2:
                     ring[side, dist + 1, piece].start()
                 across[side, dist, piece].start()
                 if turn_ == 3:
                     twin[side, dist, 0].start()
             meanwhile(dist, turn_)
+    wait_ring(4, 0)
     for piece in (0, 2):
-        ring[piece // 2, 4, piece].wait_recv()
         across[0, 4, piece].start()
     meanwhile(4, 0)
+    wait_ring(4, 1)
     for piece in (1, 3):
-        ring[piece // 2, 4, piece].wait_recv()
         across[0, 4, piece].start()
     twin[0, 4, 0].start()
     meanwhile(4, 1)
@@ -375,16 +386,15 @@
         v = pos_acc[rows, :]
         return d * jnp.concatenate([u] * 3, axis=1) - emb[rows, cols] * jnp.concatenate([v] * 3, axis=1)
 
-    rs_list = []
-
-    def rs_message(src, dst, target):
-        i = len(rs_list)
-        copy = pltpu.make_async_remote_copy(
-            src_ref=src, dst_ref=dst, send_sem=rs_send.at[i], recv_sem=rs_recv.at[i],
+    def rs_message(src, dst, target, i):
+        return pltpu.make_async_remote_copy(
+            src_ref=src, dst_ref=dst, send_sem=ag_send.at[2], recv_sem=rs_recv.at[i],
             device_id=target, device_id_type=MESH,
         )
-        rs_list.append(copy)
-        return copy
+
+    def rs_wait(i, copies):
+        part = keys.at[pl.ds(0, SUB * copies)]
+        rs_message(part, part, x_right, i).wait_recv()
 
     lane_high = lane >= 64
     mine = lane_high == (yhi == 1)
@@ -404,13 +414,13 @@
     top, bot = slice(0, FORTH // 2), slice(FORTH // 2, FORTH)
     far_right, far_left, right_bot, left_top, right_top, left_bot, cross = ([] for _ in range(7))
     for q in (0, 1):
-        far_right.append(rs_message(far_buf.at[q, 0], relay_in.at[q, 0], x_right))
-        far_left.append(rs_message(far_buf.at[q, 1], relay_in.at[q, 1], x_left))
-        right_bot.append(rs_message(near_buf.at[q, 0], side_in.at[q, 0], x_right))
-        left_top.append(rs_message(near_buf.at[q, 1], side_in.at[q, 1], x_left))
-        right_top.append(rs_message(near_buf.at[q, 2], side_in.at[q, 2], x_right))
-        left_bot.append(rs_message(near_buf.at[q, 3], side_in.at[q, 3], x_left))
-        cross.append(rs_message(cross_out.at[q], cross_in.at[q], dev_cross))
+        far_right.append(rs_message(far_buf.at[q, 0], relay_in.at[q, 0], x_right, q))
+        far_left.append(rs_message(far_buf.at[q, 1], relay_in.at[q, 1], x_left, q))
+        right_bot.append(rs_message(near_buf.at[q, 0], side_in.at[q, 0], x_right, 2 + q))
+        left_top.append(rs_message(near_buf.at[q, 1], side_in.at[q, 1], x_left, 2 + q))
+        right_top.append(rs_message(near_buf.at[q, 2], side_in.at[q, 2], x_right, 2 + q))
+        left_bot.append(rs_message(near_buf.at[q, 3], side_in.at[q, 3], x_left, 2 + q))
+        cross.append(rs_message(cross_out.at[q], cross_in.at[q], dev_cross, 4 + q))
 
     def x_far_parts(q):
         d = grad_piece(2, FORTH * q)
@@ -430,10 +440,9 @@
         hold_x[q, 1] = d[bot]
 
     def x_relay(q):
-        far_right[q].wait_recv()
+        rs_wait(q, 2)
         near_buf[q, 2] = (hold_x[q, 0] + relay_in[q, 0].astype(f32)).astype(bf16)
         right_top[q].start()
-        far_left[q].wait_recv()
         near_buf[q, 3] = (hold_x[q, 1] + relay_in[q, 1].astype(f32)).astype(bf16)
         left_bot[q].start()
 
@@ -441,8 +450,7 @@
         acc[q] = grad_piece(0, FORTH * q)
 
     def x_sum(q):
-        for copies in (right_bot, left_top, right_top, left_bot):
-            copies[q].wait_recv()
+        rs_wait(2 + q, 4)
         high = acc[q, top, :] + side_in[q, 1].astype(f32) + side_in[q, 2].astype(f32)
         low = acc[q, bot, :] + side_in[q, 0].astype(f32) + side_in[q, 3].astype(f32)
         d = jnp.concatenate([high, low], axis=0)
@@ -459,9 +467,9 @@
         half = acc[q, :, 128:256] + unpack(cross_in[q, FORTH:, :].astype(f32))
         write(FORTH * q, full, half)
 
-    y_first = [[rs_message(yo_buf.at[q, a], yi_buf.at[q, a], dev_cross) for a in range(4)] for q in (0, 1)]
+    y_first = [[rs_message(yo_buf.at[q, a], yi_buf.at[q, a], dev_cross, 6 + 4 * q + a) for a in range(4)] for q in (0, 1)]
     to = {1: x_right, 2: x_far, 3: x_left}
-    x_second = [{a: rs_message(xo_buf.at[q, a], xi_buf.at[q, a], to[a]) for a in (1, 2, 3)} for q in (0, 1)]
+    x_second = [{a: rs_message(xo_buf.at[q, a], xi_buf.at[q, a], to[a], 14 + q) for a in (1, 2, 3)} for q in (0, 1)]
 
     def y_send(q, a):
         d = grad_piece(a, HALF + FORTH * q)
@@ -486,8 +494,8 @@
 
     def y_finish(q):
         full, half = y_add(q, 0)
+        rs_wait(14 + q, 3)
         for a in (2, 1, 3):
-            x_second[q][a].wait_recv()
             full = full + xi_buf[q, a, 0:FORTH, :].astype(f32)
             half = half + unpack(xi_buf[q, a, FORTH:, :].astype(f32))
         write(HALF + FORTH * q, full, half)
@@ -527,8 +535,8 @@
     near_all.wait_send()
     far_all.wait_send()
     stat_all.wait_send()
-    for copy in messages + rs_list:
-        copy.wait_send()
+    for send, rows in ((0, 60 * SUB), (1, 64 * SUB), (2, 28 * SUB)):
+        message(0, 0, rows, sib, send, 0).wait_send()
 
 
 def shards(embeddings, partner, inv_temp):
@@ -574,12 +582,11 @@
             pltpu.VMEM((2, 4, unit, 128), bf16),
             pltpu.VMEM((2, 4, unit, 128), bf16),
             pltpu.SemaphoreType.DMA((4,)),
-            pltpu.SemaphoreType.DMA((76,)),
-            pltpu.SemaphoreType.DMA((76,)),
+            pltpu.SemaphoreType.DMA((3,)),
+            pltpu.SemaphoreType.DMA((29,)),
             pltpu.SemaphoreType.DMA((2,)),
             pltpu.SemaphoreType.DMA((4,)),
-            pltpu.SemaphoreType.DMA((28,)),
-            pltpu.SemaphoreType.DMA((28,)),
+            pltpu.SemaphoreType.DMA((16,)),
         ],
         compiler_params=pltpu.CompilerParams(
             collective_id=0, has_side_effects=True, vmem_limit_bytes=53 * 1024 * 1024

time: 63.7 us -> 62.7 us (0.984)
  Pallas kernels: 60.3 us -> 59.3 us
    pallas_call x1, Pallas kernels: 60.3 us -> 59.3 us  [shards(): pl.pallas_call(kernel, out_shape=(jax.ShapeDtypeStruct((1, ROWS), f32), j...]
where the time goes in v5:
time: 62.7 us; the launch traced here: 62.6 us
  Pallas kernels  59.3 us (95%)
  local copies, waits for them, and re-layouts  2 us (3%)
  between operations  1.29 us (2%)
    pallas_call x1, Pallas kernels, shards(): pl.pallas_call(kernel, out_shape=(jax.ShapeDtypeStruct((1, ROWS), f32), j...  59.3 us
    unnamed x4, local copies, waits for them, and re-layouts  2 us

profile of v5, /device:TPU:1, one launch (start us, length us, event | category | flops | bytes accessed | tf_op | source)
XLA Modules:
  0.0 62.6 jit_solution(6336968963838539710)
XLA Ops:
  1.3 0.0 copy-start
  1.3 0.7 %copy-done = s32[512]{0:T(512)S(1)} copy-done((s32[512]{0:T(512)S(1)}, s32[512]{0:T(512)}, u32[]{:S(2)}) %copy-start) | copy-done | bytes 2072
  2.0 59.3 %shard_map.50 = (f32[1,512]{1,0:T(1,128)S(1)}, f32[192,512]{1,0:T(8,128)S(1)}) custom-call(s32[1]{0:T(128)S(6)} %copy.7.temp_ref, s32[1,512]{1,0:T(1,128)S(1)} %bitcast.4, f32[512,1536]{1,0:T(8,128)} %emb_hbm.1), custom_call_target="tpu_custom_call" | custom-call | tf_op jit(solution)/shard_map/pallas_call | solution.py:546
  61.3 0.6 copy.8
  61.9 0.7 %copy.9 = f32[512,192]{0,1:T(8,128)} copy(f32[512,192]{0,1:T(8,128)S(1)} %bitcast.3) | data formatting | bytes 786432
Async XLA Ops:
  1.3 0.7 %copy-start = (s32[512]{0:T(512)S(1)}, s32[512]{0:T(512)}, u32[]{:S(2)}) copy-start(s32[512]{0:T(512)} %param.4) | copy-start | bytes 6148

commit v6 on v5

--- a/solution.py
+++ b/solution.py
@@ -179,15 +179,15 @@
         dist, side, other = TILES[tile]
         return lax.rem(z + (8 - dist if side == 0 else dist), 8), other
 
+    def tile_ids(tile):
+        zk, other = tile_place(tile)
+        yk = ylo if other == 0 else 1 - ylo
+        ck = jnp.where(lane < 64, core, 1 - core)
+        within = jnp.where(lane % 64 < 32, part_a * 32, part_b * 32 + 64) + lane % 32
+        return (((yk * 8 + zk) * 2 + ck) * ROWS + x * 128 + within).astype(jnp.float32)
+
     def key_ids(chunk):
-        ids = []
-        for tile in (2 * chunk, 2 * chunk + 1):
-            zk, other = tile_place(tile)
-            yk = ylo if other == 0 else 1 - ylo
-            ck = jnp.where(lane < 64, core, 1 - core)
-            within = jnp.where(lane % 64 < 32, part_a * 32, part_b * 32 + 64) + lane % 32
-            ids.append((((yk * 8 + zk) * 2 + ck) * ROWS + x * 128 + within).astype(jnp.float32))
-        return jnp.concatenate(ids, axis=1)
+        return jnp.concatenate([tile_ids(2 * chunk), tile_ids(2 * chunk + 1)], axis=1)
 
     def score_half(chunk, half):
         cols = slice(chunk * CHUNK, (chunk + 1) * CHUNK)
@@ -340,47 +340,33 @@
         col_total = col_total + col_far[dz]
     key_tot[...] = 1.0 / col_total
 
-    def weigh_rows(first):
-        for chunk in range(8):
-            cols = slice(chunk * CHUNK, (chunk + 1) * CHUNK)
-            ids = key_ids(chunk)
-            inv = []
-            for tile in (2 * chunk, 2 * chunk + 1):
-                zk, other = tile_place(tile)
-                inv.append(key_tot[pl.ds(other * 8 + zk, 1), :])
-            col_inv = jnp.concatenate(inv, axis=1)
-
-            def weigh(j, carry, cols=cols, ids=ids, col_inv=col_inv, chunk=chunk):
-                rows = pl.ds(pl.multiple_of(first + j * 64, 64), 64)
-                ri = row_inv[rows, :]
-                mate = mate_col[rows, :]
-                w = expon[rows, cols] * (jnp.concatenate([ri, ri], axis=1) + col_inv)
-                w = w - jnp.where(jnp.concatenate([mate, mate], axis=1) == ids, 2.0, 0.0)
+    def weigh_rows(first, count=FORTH):
+        for start in range(first, first + count, 32):
+            rows = slice(start, start + 32)
+            ri = row_inv[rows, :]
+            mate = mate_col[rows, :]
+            inner = jnp.zeros((32, 128), jnp.float32)
+            for tile in range(16):
+                cols = slice(tile * 128, (tile + 1) * 128)
+                w = expon[rows, cols] * (ri + col_inv[tile])
+                w = jnp.where(mate == ids[tile], w - 2.0, w)
                 w = w.astype(jnp.bfloat16)
                 weights[rows, cols] = w
-                inner = w.astype(jnp.float32) * scores[rows, cols]
-                inner = inner[:, :128] + inner[:, 128:]
-                if chunk == 0:
-                    sum_acc[rows, :] = inner
-                else:
-                    sum_acc[rows, :] += inner
-                return carry
-
-            lax.fori_loop(0, FORTH // 64, weigh, 0)
-
-        def coefs(j, carry):
-            rows = pl.ds(pl.multiple_of(first + j * 64, 64), 64)
+                inner += w.astype(jnp.float32) * scores[rows, cols]
             r = rinv[rows, :]
-            inner = jnp.sum(sum_acc[rows, :], axis=1, keepdims=True)
+            inner = jnp.sum(inner, axis=1, keepdims=True)
             pos_acc[rows, :] = r * r * inner
             sum_acc[rows, :] = r * temper
-            return carry
-
-        lax.fori_loop(0, FORTH // 64, coefs, 0)
-
-    def grad_piece(ahead, first):
+
+    ids, col_inv = [], []
+    for tile in range(16):
+        zk, other = tile_place(tile)
+        ids.append(tile_ids(tile))
+        col_inv.append(key_tot[pl.ds(other * 8 + zk, 1), :])
+
+    def grad_piece(ahead, first, count=FORTH):
         cols = pl.ds(pl.multiple_of(lax.rem(x + ahead, 4) * QUART, QUART), QUART)
-        rows = pl.ds(first, FORTH)
+        rows = pl.ds(first, count)
         d = jnp.dot(weights[rows, :], keys[:, cols], preferred_element_type=jnp.float32)
         u = sum_acc[rows, :]
         v = pos_acc[rows, :]

time: 62.7 us -> 61.7 us (0.984)
  Pallas kernels: 59.3 us -> 57.8 us
    pallas_call x1, Pallas kernels: 59.3 us -> 57.8 us  [shards(): pl.pallas_call(kernel, out_shape=(jax.ShapeDtypeStruct((1, ROWS), f32), j...]
where the time goes in v6:
time: 61.7 us; the launch traced here: 61.1 us
  Pallas kernels  57.8 us (94%)
  local copies, waits for them, and re-layouts  2 us (3%)
  between operations  1.29 us (2%)
    pallas_call x1, Pallas kernels, shards(): pl.pallas_call(kernel, out_shape=(jax.ShapeDtypeStruct((1, ROWS), f32), j...  57.8 us
    unnamed x4, local copies, waits for them, and re-layouts  2 us

profile of v6, /device:TPU:1, one launch (start us, length us, event | category | flops | bytes accessed | tf_op | source)
XLA Modules:
  0.0 61.1 jit_solution(13090959569650097065)
XLA Ops:
  1.3 0.0 copy-start
  1.3 0.7 %copy-done = s32[512]{0:T(512)S(1)} copy-done((s32[512]{0:T(512)S(1)}, s32[512]{0:T(512)}, u32[]{:S(2)}) %copy-start) | copy-done | bytes 2072
  2.0 57.8 %shard_map.50 = (f32[1,512]{1,0:T(1,128)S(1)}, f32[192,512]{1,0:T(8,128)S(1)}) custom-call(s32[1]{0:T(128)S(6)} %copy.7.temp_ref, s32[1,512]{1,0:T(1,128)S(1)} %bitcast.4, f32[512,1536]{1,0:T(8,128)} %emb_hbm.1), custom_call_target="tpu_custom_call" | custom-call | tf_op jit(solution)/shard_map/pallas_call | solution.py:532
  59.8 0.6 copy.8
  60.4 0.7 %copy.9 = f32[512,192]{0,1:T(8,128)} copy(f32[512,192]{0,1:T(8,128)S(1)} %bitcast.3) | data formatting | bytes 786432
Async XLA Ops:
  1.3 0.7 %copy-start = (s32[512]{0:T(512)S(1)}, s32[512]{0:T(512)}, u32[]{:S(2)}) copy-start(s32[512]{0:T(512)} %param.4) | copy-start | bytes 6148

commit v7 on v6

--- a/solution.py
+++ b/solution.py
@@ -490,21 +490,21 @@
     x_far_parts(0)
     weigh_rows(HALF)
     y_send(0, 2)
-    y_send(0, 1)
     weigh_rows(FORTH)
     x_far_parts(1)
+    y_send(0, 1)
     x_near_parts(0)
-    y_send(0, 3)
-    x_relay(0)
     weigh_rows(HALF + FORTH)
     y_send(1, 2)
+    x_relay(0)
+    y_send(0, 3)
     x_near_parts(1)
+    y_send(1, 1)
     x_relay(1)
-    y_send(1, 1)
     y_send(1, 3)
     y_send(0, 0)
+    x_own(0)
     y_send(1, 0)
-    x_own(0)
     x_sum(0)
     y_then_x(0, 2)
     x_own(1)

time: 61.7 us -> 61.4 us (level)
  no operation moved by 1% of the time
where the time goes in v7:
time: 61.4 us; the launch traced here: 60.9 us
  Pallas kernels  57.6 us (94%)
  local copies, waits for them, and re-layouts  2 us (3%)
  between operations  1.29 us (2%)
    pallas_call x1, Pallas kernels, shards(): pl.pallas_call(kernel, out_shape=(jax.ShapeDtypeStruct((1, ROWS), f32), j...  57.6 us
    unnamed x4, local copies, waits for them, and re-layouts  2 us

profile of v7, /device:TPU:1, one launch (start us, length us, event | category | flops | bytes accessed | tf_op | source)
XLA Modules:
  0.0 60.9 jit_solution(748032611391969322)
XLA Ops:
  1.3 0.0 copy-start
  1.3 0.7 %copy-done = s32[512]{0:T(512)S(1)} copy-done((s32[512]{0:T(512)S(1)}, s32[512]{0:T(512)}, u32[]{:S(2)}) %copy-start) | copy-done | bytes 2072
  2.0 57.6 %shard_map.50 = (f32[1,512]{1,0:T(1,128)S(1)}, f32[192,512]{1,0:T(8,128)S(1)}) custom-call(s32[1]{0:T(128)S(6)} %copy.7.temp_ref, s32[1,512]{1,0:T(1,128)S(1)} %bitcast.4, f32[512,1536]{1,0:T(8,128)} %emb_hbm.1), custom_call_target="tpu_custom_call" | custom-call | tf_op jit(solution)/shard_map/pallas_call | solution.py:532
  59.5 0.6 copy.8
  60.1 0.7 %copy.9 = f32[512,192]{0,1:T(8,128)} copy(f32[512,192]{0,1:T(8,128)S(1)} %bitcast.3) | data formatting | bytes 786432
Async XLA Ops:
  1.3 0.7 %copy-start = (s32[512]{0:T(512)S(1)}, s32[512]{0:T(512)}, u32[]{:S(2)}) copy-start(s32[512]{0:T(512)} %param.4) | copy-start | bytes 6148

commit v8 on v7

--- a/solution.py
+++ b/solution.py
@@ -152,6 +152,16 @@
             if dist in (0, 4) and side == 1:
                 continue
             for piece in range(4):
+                if dist == 4:
+                    across[side, dist, piece] = message(
+                        slot(3, piece // 2, 1, 0, piece),
+                        slot(4, 0, 1, 0, piece),
+                        SUB,
+                        z_right if piece < 2 else z_left,
+                        0,
+                        18,
+                    )
+                    continue
                 across[side, dist, piece] = message(
                     slot(dist, side, 0, 0, piece),
                     slot(dist, side, 1, 0, piece),
@@ -264,7 +274,8 @@
             score_half(2 * (dist - 1) - 1, 0)
         elif turn_ == 2:
             score_half(2 * (dist - 1) - 1, 1)
-            finish_across(dist - 1)
+            if dist < 4:
+                finish_across(dist - 1)
         else:
             finish_twin(dist - 1, 1)
             score_half(2 * (dist - 1), 0)
@@ -280,13 +291,12 @@
                     twin[side, dist, 0].start()
             meanwhile(dist, turn_)
     wait_ring(4, 0)
-    for piece in (0, 2):
-        across[0, 4, piece].start()
     meanwhile(4, 0)
     wait_ring(4, 1)
-    for piece in (1, 3):
+    twin[0, 4, 0].start()
+    finish_across(3)
+    for piece in ORDER:
         across[0, 4, piece].start()
-    twin[0, 4, 0].start()
     meanwhile(4, 1)
     meanwhile(4, 2)
     meanwhile(4, 3)

time: 61.4 us -> 63.2 us (1.029)
  Pallas kernels: 57.6 us -> 59.7 us
    pallas_call x1, Pallas kernels: 57.6 us -> 59.7 us  [shards(): pl.pallas_call(kernel, out_shape=(jax.ShapeDtypeStruct((1, ROWS), f32), j...]
where the time goes in v8:
time: 63.2 us; the launch traced here: 63 us
  Pallas kernels  59.7 us (94%)
  local copies, waits for them, and re-layouts  2 us (3%)
  between operations  1.29 us (2%)
    pallas_call x1, Pallas kernels, shards(): pl.pallas_call(kernel, out_shape=(jax.ShapeDtypeStruct((1, ROWS), f32), j...  59.7 us
    unnamed x4, local copies, waits for them, and re-layouts  2 us

profile of v8, /device:TPU:1, one launch (start us, length us, event | category | flops | bytes accessed | tf_op | source)
XLA Modules:
  0.0 63.0 jit_solution(15831944131728878843)
XLA Ops:
  1.3 0.0 copy-start
  1.3 0.7 %copy-done = s32[512]{0:T(512)S(1)} copy-done((s32[512]{0:T(512)S(1)}, s32[512]{0:T(512)}, u32[]{:S(2)}) %copy-start) | copy-done | bytes 2072
  2.0 59.7 %shard_map.50 = (f32[1,512]{1,0:T(1,128)S(1)}, f32[192,512]{1,0:T(8,128)S(1)}) custom-call(s32[1]{0:T(128)S(6)} %copy.7.temp_ref, s32[1,512]{1,0:T(1,128)S(1)} %bitcast.4, f32[512,1536]{1,0:T(8,128)} %emb_hbm.1), custom_call_target="tpu_custom_call" | custom-call | tf_op jit(solution)/shard_map/pallas_call | solution.py:542
  61.7 0.6 copy.8
  62.3 0.7 %copy.9 = f32[512,192]{0,1:T(8,128)} copy(f32[512,192]{0,1:T(8,128)S(1)} %bitcast.3) | data formatting | bytes 786432
Async XLA Ops:
  1.3 0.7 %copy-start = (s32[512]{0:T(512)S(1)}, s32[512]{0:T(512)}, u32[]{:S(2)}) copy-start(s32[512]{0:T(512)} %param.4) | copy-start | bytes 6148
